TPU v7x, 256 devices: a whole 4x4x8 slice. The times are simulated.
256 devices in a mesh: dp: 16 (over x, y), mp: 16 (over z, core).
Axes of the slice: x: 4, y: 4, z: 8, core: 2. Of those that a mesh axis runs over, the one named last changes fastest.
Arguments:
- pooled_in: bfloat16 [65536, 2048], P(('dp', 'mp')), may hold values from -24 to 24
- out_grad: bfloat16 [65536, 2048], P(('dp', 'mp')), may hold values from -6 to 6
- pooled_grad: bfloat16 [65536, 2048], P(('dp', 'mp')), may hold values from -6 to 6
- hot_ids: int32 [65536, 16], P(('dp', 'mp')), may hold values from 0 to 2047
- cold_owner: int32 [1048576, 1], P(('dp', 'mp')), may hold values from 0 to 255; in each aligned block of 4096 rows (0 to 4095, 4096 to 8191, ...) at most 32 rows name the same one
- cold_rows: int32 [65536, 16], P(('dp', 'mp')), may hold values from 0 to 4095
- mlp_weight: float32 [2048, 2048], P(('dp', 'mp')), may hold values from -0.125 to 0.125
- mlp_accum: float32 [2048, 2048], P(('dp', 'mp')), may hold values from 0.1 to 4
- hot_table: float32 [2048, 128], replicated, may hold values from -3 to 3
- hot_accum: float32 [2048], replicated, may hold values from 0.25 to 2048
- cold_table: float32 [1048576, 128], P(('dp', 'mp')), may hold values from -3 to 3
- cold_accum: float32 [1048576], P(('dp', 'mp')), may hold values from 0.1 to 4
Outputs:
- new_weight: float32 [2048, 2048], P(('dp', 'mp'))
- new_mlp_accum: float32 [2048, 2048], P(('dp', 'mp'))
- new_hot: float32 [2048, 128], replicated
- new_hot_accum: float32 [2048], replicated
- new_cold: float32 [1048576, 128], P(('dp', 'mp'))
- new_cold_accum: float32 [1048576], P(('dp', 'mp'))
Inputs may be any that keep to these rules, and one draw needn't show every extreme that they name: `cold_owner`: among the rows of one device no owner is named by more than 32 rows; some owner is named by exactly 32.
All inputs are finite; a program needn't handle non-finite values.
Results may differ from a plain program's by a relative error of at most 0.0003.
Values may be sent and summed in bfloat16 or wider, within the bound.
A program may use at most 128 MiB of HBM per device.

v0:
```python
import math

import jax
import jax.numpy as jnp
from jax import lax
from jax.sharding import PartitionSpec as P

learn_rate = 0.1


def adagrad_rows(table, accum, grads):
    accum_new = accum + jnp.mean(grads * grads, axis=1)
    return (table - learn_rate * grads / jnp.sqrt(accum_new)[:, None], accum_new)


def shards(
    pooled_in,
    out_grad,
    pooled_grad,
    hot_ids,
    cold_owner,
    cold_rows,
    mlp_weight,
    mlp_accum,
    hot_table,
    hot_accum,
    cold_table,
    cold_accum,
):
    size_dp = lax.axis_size("dp")
    size_mp = lax.axis_size("mp")
    devices = size_dp * size_mp
    factor = float(pooled_in.shape[0] * devices) ** (-0.5)
    product = lax.dot_general(
        pooled_in, out_grad, (((0,), (0,)), ((), ())), preferred_element_type=jnp.float32
    )
    weight_grad = lax.psum_scatter(product * factor, ("dp", "mp"), scatter_dimension=0, tiled=True)
    new_mlp_accum = mlp_accum + weight_grad * weight_grad
    new_weight = mlp_weight - learn_rate * weight_grad / jnp.sqrt(new_mlp_accum)
    emb_width = hot_table.shape[1]
    hot_count = hot_table.shape[0]
    lookup_grad = pooled_grad.reshape(-1, emb_width)
    lookups = lookup_grad.shape[0]
    hot_flat = hot_ids.reshape(-1)
    block_rows = math.gcd(lookups, 512)
    hot_index = jnp.arange(hot_count, dtype=jnp.int32)

    def add_block(step, totals):
        block_ids = lax.dynamic_slice_in_dim(hot_flat, step * block_rows, block_rows, 0)
        block_grad = lax.dynamic_slice_in_dim(lookup_grad, step * block_rows, block_rows, 0)
        onehot = (block_ids[:, None] == hot_index[None, :]).astype(jnp.bfloat16)
        return totals + lax.dot_general(
            onehot, block_grad, (((0,), (0,)), ((), ())), preferred_element_type=jnp.float32
        )

    hot_grad = lax.fori_loop(
        0, lookups // block_rows, add_block, jnp.zeros((hot_count, emb_width), jnp.float32)
    )
    hot_sum = lax.psum(hot_grad, ("dp", "mp"))
    new_hot, new_hot_accum = adagrad_rows(hot_table, hot_accum, hot_sum)
    owners = cold_owner[:, 0]
    local_rows = cold_rows.reshape(-1)
    capacity = max(2, 2 * lookups // devices)
    owner_onehot = (owners[:, None] == jnp.arange(devices, dtype=jnp.int32)[None, :]).astype(
        jnp.int32
    )
    slots = jnp.sum(jnp.cumsum(owner_onehot, axis=0) * owner_onehot, axis=1) - 1
    position = owners * capacity + slots
    send_grad = (
        jnp.zeros((devices * capacity, emb_width), jnp.bfloat16).at[position].set(lookup_grad)
    )
    send_rows = jnp.zeros((devices * capacity,), jnp.int32).at[position].set(local_rows)
    send_grad = send_grad.reshape(size_dp, size_mp, capacity, emb_width)
    send_rows = send_rows.reshape(size_dp, size_mp, capacity)
    got_grad, got_rows = (
        lax.all_to_all(
            lax.all_to_all(send_grad, "dp", split_axis=0, concat_axis=0, tiled=True),
            "mp",
            split_axis=1,
            concat_axis=1,
            tiled=True,
        ),
        lax.all_to_all(
            lax.all_to_all(send_rows, "dp", split_axis=0, concat_axis=0, tiled=True),
            "mp",
            split_axis=1,
            concat_axis=1,
            tiled=True,
        ),
    )
    cold_grad = jax.ops.segment_sum(
        got_grad.reshape(-1, emb_width).astype(jnp.float32),
        got_rows.reshape(-1),
        num_segments=cold_table.shape[0],
    )
    new_cold, new_cold_accum = adagrad_rows(cold_table, cold_accum, cold_grad)
    return (new_weight, new_mlp_accum, new_hot, new_hot_accum, new_cold, new_cold_accum)


def solution(mesh):
    placed = (
        P(("dp", "mp"), None),
        P(("dp", "mp"), None),
        P(("dp", "mp"), None),
        P(("dp", "mp"), None),
        P(("dp", "mp"), None),
        P(("dp", "mp"), None),
        P(("dp", "mp"), None),
        P(("dp", "mp"), None),
        P(),
        P(),
        P(("dp", "mp"), None),
        P(("dp", "mp")),
    )
    return jax.shard_map(
        shards,
        mesh=mesh,
        in_specs=placed,
        out_specs=(
            P(("dp", "mp"), None),
            P(("dp", "mp"), None),
            P(),
            P(),
            P(("dp", "mp"), None),
            P(("dp", "mp")),
        ),
        check_vma=False,
    )
```

profile of v0, /device:TPU:1, one launch (start us, length us, event | category | flops | bytes accessed | tf_op | source)
XLA Modules:
  0.0 1627.8 jit_solution(1585721926551690356)
XLA Ops:
  9.8 27.9 %while.14 = (s32[]{:T(128)}, f32[2048,128]{1,0:T(8,128)}, s32[4096]{0:T(1024)S(1)}, bf16[4096,128]{1,0:T(8,128)(2,1)S(1)}, s32[]{:T(128)}, /*index=5*/s32[]{:T(128)}, s32[]{:T(128)}, s32[]{:T(128)}) while((s32[]{:T(128)}, f32[2048,128]{1,0:T(8,128)}, s32[4096]{0:T(1024)S(1)}, bf16[4096,128]{1,0:T(8,128)(2,1)S(1)}, s32[]{:T(128)}, ...), condition=%wide.region_2.0_spmd.clone, body=%wide.region_1.0_spmd.clone.sunk | while | flops 270008320 | bytes 2234525 | solution.py:56
  12.3 3.6 fusion.25
  16.0 3.6 fusion.25
  19.6 3.6 fusion.25
  23.2 3.6 fusion.25
  26.9 3.6 fusion.25
  30.5 3.6 fusion.25
  34.1 3.6 fusion.25
  37.8 8.1 convolution_multiply_fusion
  49.3 2.6 broadcast_add_fusion
  51.9 4.4 copy.29
  56.5 2.9 fusion.9
  59.4 15.5 scatter_custom_fusion
  75.8 7.6 all-to-all-start
  83.4 12.5 scatter_custom_fusion.1
  95.9 6.6 all-to-all-start.2
  104.6 23.6 %all-to-all-done.2 = bf16[16,16,32,128]{3,2,1,0:T(8,128)(2,1)S(1)} async-done(((bf16[16,16,32,128]{3,2,1,0:T(8,128)(2,1)}), bf16[16,16,32,128]{3,2,1,0:T(8,128)(2,1)S(1)}, u32[]{:S(2)}, u32[]{:S(2)}) %all-to-all-start.2) | async-done | bytes 2097184 | tf_op jit(solution)/shard_map/all_to_all | solution.py:77
  128.2 13.9 all-to-all-start.1
  144.0 5.5 all-to-all-done.1
  149.5 3.9 all-to-all-start.3
  154.4 173.3 %all-reduce.2.cloned.1.call-done = f32[2048,128]{1,0:T(8,128)} async-done(((f32[2048,128]{1,0:T(8,128)}), f32[2048,128]{1,0:T(8,128)}) %all-reduce.2.cloned.1.call-update) | async-done | bytes 1048592 | tf_op jit(solution)/shard_map/psum | solution.py:59
  329.8 2.9 divide_subtract_fusion.1
  334.6 45.2 %scatter_custom_fusion.2 = f32[4096,128]{1,0:T(8,128)S(1)} fusion(s32[8192]{0:T(1024)S(1)} %reshape.84, bf16[8192,128]{1,0:T(8,128)(2,1)} %bitcast.22, f32[]{:T(128)} %constant.54.clone.1), kind=kCustom, calls=%fused_computation.11 | custom fusion | flops 2097152 | bytes 4194308 | tf_op jit(solution)/shard_map/scatter-add | solution.py:91
  383.1 1236.4 %reduce-scatter.2.cloned.1.call-done = f32[8,2048]{1,0:T(8,128)} async-done(((f32[2048,2048]{1,0:T(8,128)}), f32[8,2048]{1,0:T(8,128)}) %reduce-scatter.2.cloned.1.call-update) | async-done | bytes 65552 | tf_op jit(solution)/shard_map/reduce_scatter | solution.py:37
  (67 shorter events, 23.8 us)
Async XLA Ops:
  7.2 30.6 %copy-start = (bf16[256,2048]{1,0:T(8,128)(2,1)S(1)}, bf16[256,2048]{1,0:T(8,128)(2,1)}, u32[]{:S(2)}) copy-start(bf16[256,2048]{1,0:T(8,128)(2,1)} %param.14) | copy-start | bytes 3145732
  7.2 320.5 %all-reduce.2.cloned.1.call-start = ((), (), s32[]{:S(2)}) async-start(), calls=%async_computation.6 | async-start | bytes 2097152 | tf_op jit(solution)/shard_map/psum | solution.py:59
  9.8 28.0 %copy-start.3 = (bf16[256,2048]{1,0:T(8,128)(2,1)S(1)}, bf16[256,2048]{1,0:T(8,128)(2,1)}, u32[]{:S(2)}) copy-start(bf16[256,2048]{1,0:T(8,128)(2,1)} %param.15) | copy-start | bytes 3145732
  37.7 1581.8 %reduce-scatter.2.cloned.1.call-start = ((), (), s32[]{:S(2)}) async-start(), calls=%async_computation.5 | async-start | bytes 16842752 | tf_op jit(solution)/shard_map/reduce_scatter | solution.py:37
  45.9 0.7 copy-start.4
  47.3 1.9 copy-start.1
  51.9 4.4 copy-start.7
  75.8 20.0 %all-to-all-start = ((s32[16,1,512]{2,1,0:T(1,128)}), s32[16,1,512]{2,1,0:T(1,128)S(1)}, u32[]{:S(2)}, u32[]{:S(2)}) async-start(s32[16,1,512]{2,1,0:T(1,128)} %reshape.97), calls=%async_computation.1 | async-start | bytes 65536 | tf_op jit(solution)/shard_map/all_to_all | solution.py:84
  95.9 32.3 %all-to-all-start.2 = ((bf16[16,16,32,128]{3,2,1,0:T(8,128)(2,1)}), bf16[16,16,32,128]{3,2,1,0:T(8,128)(2,1)S(1)}, u32[]{:S(2)}, u32[]{:S(2)}) async-start(bf16[16,16,32,128]{3,2,1,0:T(8,128)(2,1)} %bitcast.21), calls=%async_computation.3 | async-start | bytes 4194304 | tf_op jit(solution)/shard_map/all_to_all | solution.py:77
  128.2 21.3 %all-to-all-start.1 = ((s32[16,1,512]{2,1,0:T(1,128)}), s32[16,1,512]{2,1,0:T(1,128)S(1)}, u32[]{:S(2)}, u32[]{:S(2)}) async-start(s32[16,1,512]{2,1,0:T(1,128)} %reshape.99), calls=%async_computation.2 | async-start | bytes 65536 | tf_op jit(solution)/shard_map/all_to_all | solution.py:83
  144.0 185.2 %copy-start.9 = (f32[2048]{0:T(1024)S(1)}, f32[2048]{0:T(1024)}, u32[]{:S(2)}) copy-start(f32[2048]{0:T(1024)} %param.23) | copy-start | bytes 24580
  149.5 183.2 %all-to-all-start.3 = ((bf16[16,16,32,128]{3,2,0,1:T(8,128)(2,1)}), bf16[16,16,32,128]{3,2,0,1:T(8,128)(2,1)S(1)}, u32[]{:S(2)}, u32[]{:S(2)}) async-start(bf16[16,16,32,128]{3,2,0,1:T(8,128)(2,1)} %copy.33), calls=%async_computation.4 | async-start | bytes 4194304 | tf_op jit(solution)/shard_map/all_to_all | solution.py:76
  379.8 0.7 copy-start.8
  379.8 1.6 copy-start.2
  381.4 1238.1 %copy-start.5 = (f32[8,2048]{1,0:T(8,128)S(1)}, f32[8,2048]{1,0:T(8,128)}, u32[]{:S(2)}) copy-start(f32[8,2048]{1,0:T(8,128)} %param.20) | copy-start | bytes 196612
  381.4 1238.1 %copy-start.6 = (f32[8,2048]{1,0:T(8,128)S(1)}, f32[8,2048]{1,0:T(8,128)}, u32[]{:S(2)}) copy-start(f32[8,2048]{1,0:T(8,128)} %param.21) | copy-start | bytes 196612
Sparse Core Ops, SparseCore 0:
  37.8 289.7 all-reduce.1
  330.3 1289.0 reduce-scatter.1
where the time goes:
time: 1630 us
  waiting for transfers between devices  1440 us (88%)
  other arithmetic  62.3 us (4%)
  local copies, waits for them, and re-layouts  45 us (3%)
  matrix products  35.3 us (2%)
  starting transfers between devices  32.1 us (2%)
    reduce_scatter x1, waiting for transfers between devices, shards(): lax.psum_scatter(product * factor, ('dp', 'mp'), scatter_dimension=0, til...  1240 us
    psum x1, waiting for transfers between devices, shards(): hot_sum = lax.psum(hot_grad, ('dp', 'mp'))  173 us
    scatter-add x1, other arithmetic, shards(): jax.ops.segment_sum(got_grad.reshape(-1, emb_width).astype(jnp.float32),...  45.2 us
  transfers between devices with their start and end apart: 6, of which 4 were waited for; matrix products, arithmetic and copies ran while one was open for 7% of the time, Pallas kernels for 0%

commit v1 on v0

v1 whole, which is shorter than its diff:
```python
import functools

import jax
import jax.numpy as jnp
from jax import lax
from jax.experimental import pallas as pl
from jax.experimental.pallas import tpu as pltpu
from jax.sharding import PartitionSpec as P

MESH = pl.DeviceIdType.MESH
RATE = 0.1
LANES = 128
F32 = jnp.float32
BF16 = jnp.bfloat16
I32 = jnp.int32
VMEM = pl.BlockSpec(memory_space=pltpu.VMEM)


def iota(shape, axis):
    return lax.broadcasted_iota(I32, shape, axis)


def onehot(rows, values):
    match = iota((rows, values.shape[1]), 0) == values
    return jnp.where(match, 1.0, 0.0).astype(BF16)


def dot(a, b):
    return lax.dot_general(a, b, (((1,), (0,)), ((), ())), preferred_element_type=F32)


def dot_t(a, b):
    return lax.dot_general(a, b, (((0,), (0,)), ((), ())), preferred_element_type=F32)


def adagrad_block(table, accum_row, grad):
    eye = iota((LANES, LANES), 0) == iota((LANES, LANES), 1)
    accum = jnp.sum(jnp.where(eye, accum_row, 0.0), axis=1, keepdims=True)
    new_accum = accum + jnp.sum(grad * grad, axis=1, keepdims=True) * (1.0 / LANES)
    new_table = table - grad * (RATE / jnp.sqrt(new_accum))
    new_row = jnp.sum(jnp.where(eye, new_accum, 0.0), axis=0, keepdims=True)
    return new_table, new_row


def bucket_kernel(cap, owner_ref, rows_ref, grad_ref, send_ref, ids_ref, rank_row, rhs, lhs):
    features, samples = owner_ref.shape
    devices = ids_ref.shape[0]
    earlier = jnp.where(
        iota((samples, samples), 0) < iota((samples, samples), 1), 1.0, 0.0
    ).astype(BF16)
    base = jnp.zeros((devices, 1), F32)
    for f in range(features):
        hot = onehot(devices, owner_ref[f : f + 1, :])
        hot32 = hot.astype(F32)
        before = dot(hot, earlier) + base
        rank_row[f : f + 1, :] = jnp.sum(hot32 * before, axis=0, keepdims=True)
        base = base + jnp.sum(hot32, axis=1, keepdims=True)
    rank_col = jnp.transpose(rank_row[...]).astype(I32)
    high = jnp.zeros((devices, LANES), F32)
    low = jnp.zeros((devices, LANES), F32)
    lane = iota((samples, LANES), 1)
    for f in range(features):
        rank = rank_col[:, f : f + 1]
        grad = grad_ref[:, f * LANES : (f + 1) * LANES]
        zero = jnp.zeros_like(grad)
        odd = jnp.broadcast_to(rank, (samples, LANES)) % 2 == 1
        rhs[f * samples : (f + 1) * samples, :LANES] = jnp.where(odd, zero, grad)
        rhs[f * samples : (f + 1) * samples, LANES:] = jnp.where(odd, grad, zero)
        row = rows_ref[:, f : f + 1]
        at = lane == rank
        hot = onehot(devices, owner_ref[f : f + 1, :])
        high += dot(hot, jnp.where(at, (row // 64 + 1).astype(F32), 0.0).astype(BF16))
        low += dot(hot, jnp.where(at, (row % 64).astype(F32), 0.0).astype(BF16))
    ids_ref[...] = (high * 64.0 + low - 64.0).astype(I32)
    slots = owner_ref[...] * (cap // 2) + rank_row[...].astype(I32) // 2
    step = samples

    def block(m, _):
        for f in range(features):
            lhs[:, f * samples : (f + 1) * samples] = onehot(step, slots[f : f + 1, :] - m * step)
        send_ref[pl.ds(m * step, step), :] = dot(lhs[...], rhs[...]).astype(BF16)
        return 0

    lax.fori_loop(0, send_ref.shape[0] // step, block, 0)


def hot_kernel(row_ref, col_ref, grad_ref, out_ref, rhs, lhs):
    features, samples = row_ref.shape
    half = out_ref.shape[0]
    for f in range(features):
        grad = grad_ref[:, f * LANES : (f + 1) * LANES]
        zero = jnp.zeros_like(grad)
        upper = jnp.broadcast_to(col_ref[:, f : f + 1], (samples, LANES)) >= half
        rhs[f * samples : (f + 1) * samples, :LANES] = jnp.where(upper, zero, grad)
        rhs[f * samples : (f + 1) * samples, LANES:] = jnp.where(upper, grad, zero)
    ids = row_ref[...]
    ids = jnp.where(ids >= half, ids - half, ids)
    step = samples

    def block(m, _):
        for f in range(features):
            lhs[:, f * samples : (f + 1) * samples] = onehot(step, ids[f : f + 1, :] - m * step)
        out_ref[pl.ds(m * step, step), :] = dot(lhs[...], rhs[...])
        return 0

    lax.fori_loop(0, half // step, block, 0)


def apply_kernel(row_ref, col_ref, grad_ref, table_ref, accum_ref, out_ref, new_accum_ref, rhs, lhs):
    slots = grad_ref.shape[0]
    half = table_ref.shape[0] // 2
    piece = 512
    for k in range(2):
        for i in range(0, slots, piece):
            grad = grad_ref[i : i + piece, k * LANES : (k + 1) * LANES]
            zero = jnp.zeros_like(grad)
            upper = jnp.broadcast_to(col_ref[i : i + piece, k : k + 1], (piece, LANES)) >= half
            at = k * slots + i
            rhs[at : at + piece, :LANES] = jnp.where(upper, zero, grad)
            rhs[at : at + piece, LANES:] = jnp.where(upper, grad, zero)
    step = 256

    def block(m, _):
        for k in range(2):
            for i in range(0, slots, piece):
                ids = row_ref[k : k + 1, i : i + piece]
                ids = jnp.where(ids >= half, ids - half, ids)
                at = k * slots + i
                lhs[:, at : at + piece] = onehot(step, ids - m * step)
        total = dot(lhs[...], rhs[...])
        for upper in range(2):
            for part in range(step // LANES):
                row = upper * half + m * step + part * LANES
                line = upper * (half // LANES) + m * (step // LANES) + part
                grad = total[part * LANES : (part + 1) * LANES, upper * LANES : (upper + 1) * LANES]
                table, accum = adagrad_block(
                    table_ref[pl.ds(row, LANES), :], accum_ref[pl.ds(line, 1), :], grad
                )
                out_ref[pl.ds(row, LANES), :] = table
                new_accum_ref[pl.ds(line, 1), :] = accum
        return 0

    lax.fori_loop(0, half // step, block, 0)


def reduce_kernel(
    nx, ny, nz, factor,
    x_ref, g_ref, hot_ref, w_ref, a_ref, ht_ref, ha_ref,
    nw_ref, na_ref, nh_ref, nha_ref,
    xp, gp, hp, prod, recv1, recv2, sums, recv3, total, last, hx, hy, hz, hsum, ss, rs,
):
    dp, mp = lax.axis_index("dp"), lax.axis_index("mp")
    x, y = lax.div(dp, ny), lax.rem(dp, ny)
    z, c = lax.div(mp, 2), lax.rem(mp, 2)

    def at_x(j):
        return (lax.rem(x + j, nx) * ny + y, mp)

    def at_y(j):
        return (x * ny + lax.rem(y + j, ny), mp)

    def at_z(j):
        return (dp, lax.rem(z + j, nz) * 2 + c)

    partner = (dp, z * 2 + 1 - c)
    barrier = pltpu.get_barrier_semaphore()
    peers = [partner]
    peers += [at_x(j) for j in range(1, nx)] + [at_y(j) for j in range(1, ny)]
    peers += [at_z(j) for j in range(1, nz)]
    for peer in peers:
        pl.semaphore_signal(barrier, inc=1, device_id=peer, device_id_type=MESH)
    pl.semaphore_wait(barrier, len(peers))

    copies = []

    def send(src, dst, device):
        k = len(copies)
        copy = pltpu.make_async_remote_copy(
            src_ref=src, dst_ref=dst, send_sem=ss.at[k], recv_sem=rs.at[k],
            device_id=device, device_id_type=MESH,
        )
        copy.start()
        copies.append(copy)
        return copy

    half = g_ref.shape[1] // 2
    quarter = half // 2
    rows = x_ref.shape[1]
    got_g = send(g_ref.at[:, pl.ds(pl.multiple_of((1 - c) * half, half), half)], gp, partner)
    got_x = send(x_ref, xp, partner)
    got_h = send(hot_ref.at[:, pl.ds(pl.multiple_of((1 - c) * LANES, LANES), LANES)], hp, partner)
    got_g.wait_recv()
    got_x.wait_recv()

    n = (nx, ny)
    chunk = rows // nx
    tile = rows // (nx * ny)
    here = (x, y)

    def compute(h, rel):
        dest = lax.rem(here[h] + rel, n[h])
        cols = pl.ds(pl.multiple_of(c * half + h * quarter, quarter), quarter)
        for t in range(chunk // tile):
            if h == 0:
                at = dest * chunk + t * tile
            else:
                at = t * (rows // nx) + dest * tile
            at = pl.ds(pl.multiple_of(at, LANES), tile)
            prod[h, rel, t * tile : (t + 1) * tile, :] = dot_t(x_ref[:, at], g_ref[:, cols]) + dot_t(
                xp[:, at], gp[:, h * quarter : (h + 1) * quarter]
            )

    def ring_far(part, buf, up, down, size):
        a, b = (0, size // 2), (size // 2, size // 2)
        return send(part(2, *a), buf.at[0], up), send(part(2, *b), buf.at[1], down)

    def ring_near(part, buf, up, down, size):
        a, b = (0, size // 2), (size // 2, size // 2)
        return send(part(1, *b), buf.at[2], up), send(part(3, *a), buf.at[3], down)

    def ring_join(part, buf, up, down, size, far):
        a, b = (0, size // 2), (size // 2, size // 2)
        far[0].wait_recv()
        ref = part(1, *a)
        ref[...] = ref[...] + buf[0]
        one = send(ref, buf.at[4], up)
        far[1].wait_recv()
        ref = part(3, *b)
        ref[...] = ref[...] + buf[1]
        return one, send(ref, buf.at[5], down)

    def ring_end(part, buf, size, near, join):
        a, b = (0, size // 2), (size // 2, size // 2)
        for copy in near + join:
            copy.wait_recv()
        ref = part(0, *a)
        ref[...] = ref[...] + buf[3] + buf[4]
        ref = part(0, *b)
        ref[...] = ref[...] + buf[2] + buf[5]

    def part1(h):
        return lambda rel, start, size: prod.at[h, rel, pl.ds(start, size)]

    def part2(h):
        def part(rel, start, size):
            dest = lax.rem(here[1 - h] + rel, n[1 - h])
            return prod.at[h, 0, pl.ds(pl.multiple_of(dest * tile + start, 8), size)]

        return part

    ends = ((at_x(1), at_x(nx - 1)), (at_y(1), at_y(ny - 1)))
    far, near, join = [], [], []
    for h in range(2):
        compute(h, 2)
        far.append(ring_far(part1(h), recv1.at[h], *ends[h], chunk))
    for h in range(2):
        compute(h, 1)
        compute(h, 3)
        near.append(ring_near(part1(h), recv1.at[h], *ends[h], chunk))

    hot_rows = hp.shape[0]
    mine = pl.ds(pl.multiple_of(c * LANES, LANES), LANES)
    got_h.wait_recv()
    hp[...] = hp[...] + hot_ref[:, mine]
    hrx, hry, hrz = hot_rows // nx, hot_rows // (nx * ny), hot_rows // (nx * ny * nz)
    hots = [
        send(hp.at[pl.ds(pl.multiple_of(lax.rem(x + j, nx) * hrx, 8), hrx)], hx.at[j - 1], at_x(j))
        for j in range(1, nx)
    ]
    for h in range(2):
        compute(h, 0)
    for copy in hots:
        copy.wait_recv()
    base_x = pl.multiple_of(x * hrx, 8)
    ref = hp.at[pl.ds(base_x, hrx)]
    ref[...] = ref[...] + hx[0] + hx[1] + hx[2]
    base_y = pl.multiple_of(base_x + y * hry, 8)
    hots = [
        send(hp.at[pl.ds(pl.multiple_of(base_x + lax.rem(y + j, ny) * hry, 8), hry)], hy.at[j - 1], at_y(j))
        for j in range(1, ny)
    ]
    for h in range(2):
        join.append(ring_join(part1(h), recv1.at[h], *ends[h], chunk, far[h]))
    for copy in hots:
        copy.wait_recv()
    ref = hp.at[pl.ds(base_y, hry)]
    ref[...] = ref[...] + hy[0] + hy[1] + hy[2]
    base_z = pl.multiple_of(base_y + z * hrz, 8)
    hots = [
        send(hp.at[pl.ds(pl.multiple_of(base_y + lax.rem(z + j, nz) * hrz, 8), hrz)], hz.at[j - 1], at_z(j))
        for j in range(1, nz)
    ]
    for copy in hots:
        copy.wait_recv()
    got = hp[pl.ds(base_z, hrz), :]
    for j in range(1, nz):
        got = got + hz[j - 1]
    base_c = pl.multiple_of(c * hot_rows, 8)
    own_z = pl.multiple_of(base_c + base_z, 8)
    hsum[pl.ds(own_z, hrz), :] = got
    own = hsum.at[pl.ds(own_z, hrz)]
    hots = [send(own, own, at_z(j)) for j in range(1, nz)]
    for copy in hots:
        copy.wait_recv()
    own = hsum.at[pl.ds(pl.multiple_of(base_c + base_y, 8), hry)]
    hots = [send(own, own, at_y(j)) for j in range(1, ny)]
    for copy in hots:
        copy.wait_recv()
    own = hsum.at[pl.ds(pl.multiple_of(base_c + base_x, 8), hrx)]
    hots = [send(own, own, at_x(j)) for j in range(1, nx)]
    for copy in hots:
        copy.wait_recv()
    own = hsum.at[pl.ds(base_c, hot_rows)]
    got_hot = send(own, own, partner)

    second = (ends[1], ends[0])
    far2, near2, join2 = [], [], []
    for h in range(2):
        ring_end(part1(h), recv1.at[h], chunk, near[h], join[h])
        far2.append(ring_far(part2(h), recv2.at[h], *second[h], tile))
        near2.append(ring_near(part2(h), recv2.at[h], *second[h], tile))

    got_hot.wait_recv()
    for i in range(hsum.shape[0] // LANES):
        at = slice(i * LANES, (i + 1) * LANES)
        table, accum = adagrad_block(ht_ref[at, :], ha_ref[i : i + 1, :], hsum[at, :])
        nh_ref[at, :] = table
        nha_ref[i : i + 1, :] = accum

    for h in range(2):
        join2.append(ring_join(part2(h), recv2.at[h], *second[h], tile, far2[h]))
    for h in range(2):
        ring_end(part2(h), recv2.at[h], tile, near2[h], join2[h])
        at = pl.multiple_of(here[1 - h] * tile, 8)
        sums[:, h * quarter : (h + 1) * quarter] = prod[h, 0, pl.ds(at, tile), :]
    band = tile // nz
    gots = [
        send(sums.at[pl.ds(pl.multiple_of(lax.rem(z + j, nz) * band, 8), band)], recv3.at[j - 1], at_z(j))
        for j in range(1, nz)
    ]
    value = sums[pl.ds(pl.multiple_of(z * band, 8), band), :]
    for j in range(1, nz):
        gots[j - 1].wait_recv()
        value = value + recv3[j - 1]
    total[...] = value
    out_rows = band // 2
    got = send(total.at[pl.ds(pl.multiple_of((1 - c) * out_rows, 8), out_rows)], last, partner)
    got.wait_recv()
    own = total[pl.ds(pl.multiple_of(c * out_rows, 8), out_rows), :]
    other = last[...]
    for side in range(2):
        cols = slice(side * half, (side + 1) * half)
        grad = jnp.where(c == side, own, other) * factor
        accum = a_ref[:, cols] + grad * grad
        na_ref[:, cols] = accum
        nw_ref[:, cols] = w_ref[:, cols] - RATE * grad / jnp.sqrt(accum)
    for copy in copies:
        copy.wait_send()


def shards(
    nx, ny, nz,
    pooled_in, out_grad, pooled_grad, hot_ids, cold_owner, cold_rows,
    mlp_weight, mlp_accum, hot_table, hot_accum, cold_table, cold_accum,
):
    devices = nx * ny * nz * 2
    samples, features = hot_ids.shape
    hid = pooled_in.shape[1]
    hot = hot_table.shape[0]
    rows = cold_table.shape[0]
    lookups = samples * features
    cap = 2 * lookups // devices
    slots = devices * cap // 2
    params = functools.partial(pltpu.CompilerParams, vmem_limit_bytes=48 << 20)

    owner_row = cold_owner.reshape(samples, features).T
    send_grad, ids = pl.pallas_call(
        functools.partial(bucket_kernel, cap),
        out_shape=(
            jax.ShapeDtypeStruct((slots, 2 * LANES), BF16),
            jax.ShapeDtypeStruct((devices, LANES), I32),
        ),
        in_specs=[VMEM] * 3,
        out_specs=(VMEM, VMEM),
        scratch_shapes=[
            pltpu.VMEM((features, samples), F32),
            pltpu.VMEM((lookups, 2 * LANES), BF16),
            pltpu.VMEM((samples, lookups), BF16),
        ],
        compiler_params=params(),
        name="bucket",
    )(owner_row, cold_rows, pooled_grad)
    got_ids = lax.all_to_all(ids[:, :cap], ("dp", "mp"), split_axis=0, concat_axis=0, tiled=True)
    got_grad = lax.all_to_all(
        send_grad.reshape(devices, cap // 2, 2 * LANES), ("dp", "mp"), split_axis=0, concat_axis=0, tiled=True
    ).reshape(slots, 2 * LANES)

    hot_part = pl.pallas_call(
        hot_kernel,
        out_shape=jax.ShapeDtypeStruct((hot // 2, 2 * LANES), F32),
        in_specs=[VMEM] * 3,
        out_specs=VMEM,
        scratch_shapes=[
            pltpu.VMEM((lookups, 2 * LANES), BF16),
            pltpu.VMEM((samples, lookups), BF16),
        ],
        compiler_params=params(),
        name="hot",
    )(hot_ids.T, hot_ids, pooled_grad)

    quarter = hid // 4
    chunk, tile = hid // nx, hid // (nx * ny)
    band = tile // nz
    half_hot = hot // 2
    hrx, hry, hrz = half_hot // nx, half_hot // (nx * ny), half_hot // (nx * ny * nz)
    n_copies = 3 + 2 * 6 * 2 + (nz - 1) + 1 + 2 * (nx - 1 + ny - 1 + nz - 1) + 1
    new_weight, new_mlp_accum, new_hot, new_hot_accum = pl.pallas_call(
        functools.partial(reduce_kernel, nx, ny, nz, float(samples * devices) ** (-0.5)),
        out_shape=(
            jax.ShapeDtypeStruct(mlp_weight.shape, F32),
            jax.ShapeDtypeStruct(mlp_accum.shape, F32),
            jax.ShapeDtypeStruct(hot_table.shape, F32),
            jax.ShapeDtypeStruct((hot // LANES, LANES), F32),
        ),
        in_specs=[VMEM] * 7,
        out_specs=(VMEM,) * 4,
        scratch_shapes=[
            pltpu.VMEM((samples, hid), BF16),
            pltpu.VMEM((samples, hid // 2), BF16),
            pltpu.VMEM((half_hot, LANES), F32),
            pltpu.VMEM((2, 4, chunk, quarter), F32),
            pltpu.VMEM((2, 6, chunk // 2, quarter), F32),
            pltpu.VMEM((2, 6, tile // 2, quarter), F32),
            pltpu.VMEM((tile, hid // 2), F32),
            pltpu.VMEM((nz - 1, band, hid // 2), F32),
            pltpu.VMEM((band, hid // 2), F32),
            pltpu.VMEM((band // 2, hid // 2), F32),
            pltpu.VMEM((nx - 1, hrx, LANES), F32),
            pltpu.VMEM((ny - 1, hry, LANES), F32),
            pltpu.VMEM((nz - 1, hrz, LANES), F32),
            pltpu.VMEM((hot, LANES), F32),
            pltpu.SemaphoreType.DMA((n_copies,)),
            pltpu.SemaphoreType.DMA((n_copies,)),
        ],
        compiler_params=params(collective_id=0, has_side_effects=True),
        name="reduce",
    )(
        pooled_in, out_grad, hot_part, mlp_weight, mlp_accum, hot_table,
        hot_accum.reshape(hot // LANES, LANES),
    )

    id_col = got_ids.reshape(slots, 2)
    new_cold, new_cold_accum = pl.pallas_call(
        apply_kernel,
        out_shape=(
            jax.ShapeDtypeStruct(cold_table.shape, F32),
            jax.ShapeDtypeStruct((rows // LANES, LANES), F32),
        ),
        in_specs=[VMEM] * 5,
        out_specs=(VMEM, VMEM),
        scratch_shapes=[
            pltpu.VMEM((2 * slots, 2 * LANES), BF16),
            pltpu.VMEM((256, 2 * slots), BF16),
        ],
        compiler_params=params(),
        name="apply",
    )(id_col.T, id_col, got_grad, cold_table, cold_accum.reshape(rows // LANES, LANES))
    return (
        new_weight,
        new_mlp_accum,
        new_hot,
        new_hot_accum.reshape(hot),
        new_cold,
        new_cold_accum.reshape(rows),
    )


def solution(mesh):
    split = P(("dp", "mp"), None)
    nx = ny = 4
    nz = mesh.shape["mp"] // 2
    return jax.shard_map(
        functools.partial(shards, nx, ny, nz),
        mesh=mesh,
        in_specs=(split,) * 8 + (P(), P(), split, P(("dp", "mp"))),
        out_specs=(split, split, P(), P(), split, P(("dp", "mp"))),
        check_vma=False,
    )
```

time: 1630 us -> 190 us (0.12)
  waiting for transfers between devices: 1440 us -> 0.01 us
  Pallas kernels: 0 us -> 141 us
  other arithmetic: 62.3 us -> 2.37 us
  local copies, waits for them, and re-layouts: 45 us -> 8.66 us
  matrix products: 35.3 us -> 0 us
  blocking collectives: 0 us -> 29.1 us
  starting transfers between devices: 32.1 us -> 7.35 us
    reduce_scatter x1 -> x0, waiting for transfers between devices: 1240 us -> none  [shards(): lax.psum_scatter(product * factor, ('dp', 'mp'), scatter_dimension=0, til...]
    psum x1 -> x0, waiting for transfers between devices: 173 us -> none  [shards(): hot_sum = lax.psum(hot_grad, ('dp', 'mp'))]
    pallas_call x0 -> x4, Pallas kernels: none -> 141 us  [the longest x1 104 us: shards(): pl.pallas_call(functools.partial(reduce_kernel, nx, ny, nz, float(samples...]
    scatter-add x1 -> x0, other arithmetic: 45.2 us -> none  [shards(): jax.ops.segment_sum(got_grad.reshape(-1, emb_width).astype(jnp.float32),...]
    dot_general x9 -> x0, matrix products: 35.3 us -> none  [the longest x8 27.2 us: add_block(): lax.dot_general(onehot, block_grad, (((0,), (0,)), ((), ())), preferred_e...]
    all_to_all x4 -> x1, waiting for transfers between devices: 29.1 us -> 0.01 us  [shards(): lax.all_to_all(send_grad.reshape(devices, cap // 2, 2 * LANES), ('dp', 'm...]
    all_to_all x0 -> x1, blocking collectives: none -> 29.1 us  [shards(): lax.all_to_all(ids[:, :cap], ('dp', 'mp'), split_axis=0, concat_axis=0, t...]
    scatter x2 -> x0, local copies, waits for them, and re-layouts: 28 us -> none  [the longest x1 15.5 us: shards(): jnp.zeros((devices * capacity,), jnp.int32).at[position].set(local_rows)]
  transfers between devices with their start and end apart: 6 -> 1, of which waited for: 4 -> 0; matrix products, arithmetic and copies ran while one was open for 7% -> 1% of each run, Pallas kernels for 0% -> 57%
where the time goes in v1:
time: 190 us
  Pallas kernels  141 us (74%)
  blocking collectives  29.1 us (15%)
  local copies, waits for them, and re-layouts  8.66 us (5%)
  starting transfers between devices  7.35 us (4%)
  other arithmetic  2.37 us (1%)
    pallas_call x1, Pallas kernels, shards(): pl.pallas_call(functools.partial(reduce_kernel, nx, ny, nz, float(samples...  104 us
    all_to_all x1, blocking collectives, shards(): lax.all_to_all(ids[:, :cap], ('dp', 'mp'), split_axis=0, concat_axis=0, t...  29.1 us
    pallas_call x1, Pallas kernels, shards(): pl.pallas_call(functools.partial(bucket_kernel, cap), out_shape=(jax.Shap...  18.2 us
    pallas_call x1, Pallas kernels, shards(): pl.pallas_call(apply_kernel, out_shape=(jax.ShapeDtypeStruct(cold_table.s...  15.9 us
    all_to_all x1, starting transfers between devices, shards(): lax.all_to_all(send_grad.reshape(devices, cap // 2, 2 * LANES), ('dp', 'm...  7.35 us
    unnamed x29, local copies, waits for them, and re-layouts  6.76 us
  transfers between devices with their start and end apart: 1, of which 0 were waited for; matrix products, arithmetic and copies ran while one was open for 1% of the time, Pallas kernels for 57%

profile of v1, /device:TPU:1, one launch (start us, length us, event | category | flops | bytes accessed | tf_op | source)
XLA Modules:
  0.0 189.6 jit_solution(1487632351014484105)
XLA Ops:
  0.6 0.5 broadcast.6
  1.1 1.4 reduce.7
  2.5 0.1 reshape.41
  2.6 0.1 copy.26
  2.7 0.8 copy.27.rows_ref
  3.5 1.2 copy-done
  4.8 18.2 %bucket.1 = (bf16[4096,256]{1,0:T(8,128)(2,1)}, s32[256,128]{1,0:T(8,128)S(1)}) custom-call(s32[16,256]{1,0:T(8,128)S(1)} %bitcast.17, s32[256,16]{1,0:T(8,128)S(1)} %copy.27.rows_ref, bf16[256,2048]{1,0:T(8,128)(2,1)S(1)} %copy-done), custom_call_target="tpu_custom_call" | custom-call | tf_op jit(solution)/shard_map/bucket/pallas_call | solution.py:377
  23.0 29.1 %all_to_all.14 = s32[256,1,32]{2,1,0:T(1,128)} all-to-all(s32[256,1,32]{2,1,0:T(1,128)S(1)} %bitcast.15), channel_id=1, replica_groups=mesh['dp'=16,'mp'=16] {'dp','mp'}, dimensions={0} | all-to-all | bytes 65536 | tf_op jit(solution)/shard_map/all_to_all | solution.py:393
  52.0 7.4 %all-to-all-start.1 = ((bf16[256,16,256]{2,1,0:T(8,128)(2,1)}), bf16[256,16,256]{2,1,0:T(8,128)(2,1)}, u32[]{:S(2)}, u32[]{:S(2)}) async-start(bf16[256,16,256]{2,1,0:T(8,128)(2,1)} %bitcast.7), calls=%async_computation.1 | async-start | bytes 4194304 | tf_op jit(solution)/shard_map/all_to_all | solution.py:394
  59.4 0.0 copy-start.5
  59.4 0.0 copy-start.6
  59.4 0.1 copy.25.col_ref
  59.5 3.5 %hot.1.hot_ref = f32[1024,256]{1,0:T(8,128)S(1)} custom-call(s32[16,256]{1,0:T(8,128)S(1)} %bitcast.16, s32[256,16]{1,0:T(8,128)S(1)} %copy.25.col_ref, bf16[256,2048]{1,0:T(8,128)(2,1)S(1)} %copy-done.1), custom_call_target="tpu_custom_call" | custom-call | tf_op jit(solution)/shard_map/hot/pallas_call | solution.py:398
  63.1 0.0 copy-start.4
  63.1 1.2 copy-done.4
  64.3 103.8 %reduce.9 = (f32[8,2048]{1,0:T(8,128)S(1)}, f32[8,2048]{1,0:T(8,128)S(1)}, f32[2048,128]{1,0:T(8,128)S(1)}, f32[16,128]{1,0:T(8,128)S(1)}) custom-call(bf16[256,2048]{1,0:T(8,128)(2,1)S(1)} %copy-done.2, bf16[256,2048]{1,0:T(8,128)(2,1)S(1)} %copy-done.3, f32[1024,256]{1,0:T(8,128)S(1)} %hot.1.hot_ref, f32[8,2048]{1,0:T(8,128)S(1)} %copy-done.5, ...), custom_call_target="tpu_custom_call" | custom-call | tf_op jit(solution)/shard_map/reduce/pallas_call | solution.py:417
  168.1 1.0 reduce.8
  169.1 1.1 reshape.42.col_ref
  170.2 0.6 copy.29
  170.9 15.9 %apply.1 = (f32[4096,128]{1,0:T(8,128)}, f32[32,128]{1,0:T(8,128)}) custom-call(s32[2,4096]{1,0:T(2,128)S(1)} %bitcast.14, s32[4096,2]{1,0:T(8,128)S(1)} %reshape.42.col_ref, bf16[4096,256]{1,0:T(8,128)(2,1)} %bitcast.8.grad_ref, f32[4096,128]{1,0:T(8,128)} %table_ref.1, f32[32,128]{1,0:T(8,128)S(1)} %bitcast.18), custom_call_target="tpu_custom_call" | custom-call | tf_op jit(solution)/shard_map/apply/pallas_call | solution.py:453
  186.8 0.6 copy.34
  187.4 0.6 copy.35
  188.0 1.0 copy.36
  189.0 0.6 copy.37
  (18 shorter events, 0.0 us)
Async XLA Ops:
  3.5 1.2 copy-start
  52.0 7.4 %copy-start.7 = (s32[256,16]{0,1:T(8,128)S(1)}, s32[256,16]{0,1:T(8,128)}, u32[]{:S(2)}) copy-start(s32[256,16]{0,1:T(8,128)} %param.15) | copy-start | bytes 49156
  52.0 7.5 %copy-start.1 = (bf16[256,2048]{1,0:T(8,128)(2,1)S(1)}, bf16[256,2048]{1,0:T(8,128)(2,1)}, u32[]{:S(2)}) copy-start(bf16[256,2048]{1,0:T(8,128)(2,1)} %grad_ref.3) | copy-start | bytes 3145732
  52.0 118.9 %all-to-all-start.1 = ((bf16[256,16,256]{2,1,0:T(8,128)(2,1)}), bf16[256,16,256]{2,1,0:T(8,128)(2,1)}, u32[]{:S(2)}, u32[]{:S(2)}) async-start(bf16[256,16,256]{2,1,0:T(8,128)(2,1)} %bitcast.7), calls=%async_computation.1 | async-start | bytes 4194304 | tf_op jit(solution)/shard_map/all_to_all | solution.py:394
  59.4 3.6 %copy-start.2 = (bf16[256,2048]{1,0:T(8,128)(2,1)S(1)}, bf16[256,2048]{1,0:T(8,128)(2,1)}, u32[]{:S(2)}) copy-start(bf16[256,2048]{1,0:T(8,128)(2,1)} %x_ref.1) | copy-start | bytes 3145732
  59.4 3.6 %copy-start.5 = (f32[8,2048]{1,0:T(8,128)S(1)}, f32[8,2048]{1,0:T(8,128)}, u32[]{:S(2)}) copy-start(f32[8,2048]{1,0:T(8,128)} %w_ref.1) | copy-start | bytes 196612
  59.4 3.6 %copy-start.6 = (f32[8,2048]{1,0:T(8,128)S(1)}, f32[8,2048]{1,0:T(8,128)}, u32[]{:S(2)}) copy-start(f32[8,2048]{1,0:T(8,128)} %a_ref.1) | copy-start | bytes 196612
  59.4 3.6 %copy-start.9 = (f32[2048]{0:T(1024)S(1)}, f32[2048]{0:T(1024)}, u32[]{:S(2)}) copy-start(f32[2048]{0:T(1024)} %param.21) | copy-start | bytes 24580
  59.5 3.5 %copy-start.3 = (bf16[256,2048]{1,0:T(8,128)(2,1)S(1)}, bf16[256,2048]{1,0:T(8,128)(2,1)}, u32[]{:S(2)}) copy-start(bf16[256,2048]{1,0:T(8,128)(2,1)} %g_ref.1) | copy-start | bytes 3145732
  63.1 1.2 copy-start.4
  64.3 103.8 %copy-start.10 = (s32[256,1,32]{2,1,0:T(1,128)S(1)}, s32[256,1,32]{2,1,0:T(1,128)}, u32[]{:S(2)}) copy-start(s32[256,1,32]{2,1,0:T(1,128)} %all_to_all.14) | copy-start | bytes 98308
  169.1 1.8 copy-start.8

commit v2 on v1

v2 whole, which is shorter than its diff:
```python
import functools

import jax
import jax.numpy as jnp
from jax import lax
from jax.experimental import pallas as pl
from jax.experimental.pallas import tpu as pltpu
from jax.sharding import PartitionSpec as P

MESH = pl.DeviceIdType.MESH
RATE = 0.1
LANES = 128
F32 = jnp.float32
BF16 = jnp.bfloat16
I32 = jnp.int32
VMEM = pl.BlockSpec(memory_space=pltpu.VMEM)


def iota(shape, axis):
    return lax.broadcasted_iota(I32, shape, axis)


def onehot(rows, values):
    match = iota((rows, values.shape[1]), 0) == values
    return jnp.where(match, 1.0, 0.0).astype(BF16)


def dot(a, b):
    return lax.dot_general(a, b, (((1,), (0,)), ((), ())), preferred_element_type=F32)


def dot_t(a, b):
    return lax.dot_general(a, b, (((0,), (0,)), ((), ())), preferred_element_type=F32)


def adagrad_block(table, accum_row, grad):
    eye = iota((LANES, LANES), 0) == iota((LANES, LANES), 1)
    accum = jnp.sum(jnp.where(eye, accum_row, 0.0), axis=1, keepdims=True)
    new_accum = accum + jnp.sum(grad * grad, axis=1, keepdims=True) * (1.0 / LANES)
    new_table = table - grad * (RATE / jnp.sqrt(new_accum))
    new_row = jnp.sum(jnp.where(eye, new_accum, 0.0), axis=0, keepdims=True)
    return new_table, new_row


def dot_nt(a, b):
    return lax.dot_general(a, b, (((1,), (1,)), ((), ())), preferred_element_type=F32)


def split_columns(rhs, at, grad, upper):
    zero = jnp.zeros_like(grad)
    rows = grad.shape[0]
    rhs[at : at + rows, :LANES] = jnp.where(upper, zero, grad)
    rhs[at : at + rows, LANES:] = jnp.where(upper, grad, zero)


def step_kernel(
    nx, ny, nz, cap, factor,
    x_ref, g_ref, pg_ref, hid_ref, own_ref, row_ref, w_ref, a_ref, ht_ref, ha_ref, ct_ref, ca_ref,
    nw_ref, na_ref, nh_ref, nha_ref, nc_ref, nca_ref,
    xp, gp, prod, recv1, recv2, sums, recv3, total, last,
    hpart, hp, hx, hy, hz, hsum,
    rank_row, own_row, rhs, lhs, send_buf, mid, fin, idsend, idmid, idout, idfin, idrow, ids, arhs, alhs, cold,
    ss, rs, s1, r1, s2, r2, t1, q1, t2, q2,
):
    samples, features = hid_ref.shape
    n_dp, n_mp = nx * ny, nz * 2
    devices = n_dp * n_mp
    deep = cap // 2
    dp, mp = lax.axis_index("dp"), lax.axis_index("mp")
    x, y = lax.div(dp, ny), lax.rem(dp, ny)
    z, c = lax.div(mp, 2), lax.rem(mp, 2)

    def at_x(j):
        return (lax.rem(x + j, nx) * ny + y, mp)

    def at_y(j):
        return (x * ny + lax.rem(y + j, ny), mp)

    def at_z(j):
        return (dp, lax.rem(z + j, nz) * 2 + c)

    def at_dp(i):
        return lax.rem(x + lax.div(i, ny), nx) * ny + lax.rem(y + lax.rem(i, ny), ny)

    mid_z = nz // 2

    def at_mp(p):
        pz, pc = lax.div(p, 2), lax.rem(p, 2)
        jz = jnp.where(lax.rem(pz, 2) == 1, mid_z - lax.div(pz + 1, 2), mid_z + lax.div(pz, 2))
        return lax.rem(z + jz, nz) * 2 + lax.rem(c + pc, 2)

    here_slot = n_mp - 2
    partner = (dp, z * 2 + 1 - c)
    barrier = pltpu.get_barrier_semaphore()

    def greet_dp(i, _):
        pl.semaphore_signal(barrier, inc=1, device_id=(at_dp(i), mp), device_id_type=MESH)
        return 0

    def greet_mp(j, _):
        pl.semaphore_signal(
            barrier, inc=1, device_id=(dp, lax.rem(mp + j, n_mp)), device_id_type=MESH
        )
        return 0

    lax.fori_loop(1, n_dp, greet_dp, 0)
    lax.fori_loop(1, n_mp, greet_mp, 0)

    line = LANES // features
    spread = jnp.concatenate(
        [
            jnp.broadcast_to(own_ref[:, r * LANES : (r + 1) * LANES], (line, LANES))
            for r in range(own_ref.shape[1] // LANES)
        ],
        axis=0,
    )
    keep = iota((samples, LANES), 1) // features == iota((samples, LANES), 0) % line
    pick = jnp.where(iota((features, LANES), 1) % features == iota((features, LANES), 0), 1.0, 0.0)
    owner = dot_nt(pick.astype(BF16), jnp.where(keep, spread, 0).astype(F32).astype(BF16)).astype(I32)
    to_mp = owner % n_mp
    jz = (to_mp // 2 - z + nz) % nz
    pz = jnp.where(jz > mid_z, 2 * (jz - mid_z), jnp.maximum(2 * (mid_z - jz) - 1, 0))
    place = (pz * 2 + (to_mp + c) % 2) * n_dp + owner // n_mp
    own_row[...] = place
    earlier = jnp.where(
        iota((samples, samples), 0) < iota((samples, samples), 1), 1.0, 0.0
    ).astype(BF16)
    base = jnp.zeros((devices, 1), F32)
    for f in range(features):
        hot = onehot(devices, own_row[f : f + 1, :])
        hot32 = hot.astype(F32)
        before = dot(hot, earlier) + base
        rank_row[f : f + 1, :] = jnp.sum(hot32 * before, axis=0, keepdims=True)
        base = base + jnp.sum(hot32, axis=1, keepdims=True)

    pl.semaphore_wait(barrier, n_dp + n_mp - 2)

    copies = []

    def send(src, dst, device):
        k = len(copies)
        copy = pltpu.make_async_remote_copy(
            src_ref=src, dst_ref=dst, send_sem=ss.at[k], recv_sem=rs.at[k],
            device_id=device, device_id_type=MESH,
        )
        copy.start()
        copies.append(copy)
        return copy

    half = g_ref.shape[1] // 2
    quarter = half // 2
    rows = x_ref.shape[1]
    got_g = send(g_ref.at[:, pl.ds(pl.multiple_of((1 - c) * half, half), half)], gp, partner)
    got_x = send(x_ref, xp, partner)

    rank_col = jnp.transpose(rank_row[...]).astype(I32)
    lane = iota((samples, LANES), 1)
    numbers = jnp.zeros((devices, LANES), F32)
    for f in range(features):
        rank = jnp.broadcast_to(rank_col[:, f : f + 1], (samples, LANES))
        grad = pg_ref[:, f * LANES : (f + 1) * LANES]
        split_columns(rhs, f * samples, grad, rank % 2 == 1)
        row = jnp.broadcast_to(row_ref[:, f : f + 1], (samples, LANES))
        spot = (rank % 2) * deep + rank // 2
        digit = jnp.where(lane < cap, row // 64 + 1, row % 64)
        digit = jnp.where((lane % cap == spot) & (lane < 2 * cap), digit, 0).astype(F32).astype(BF16)
        numbers += dot(onehot(devices, own_row[f : f + 1, :]), digit)
    idsend[...] = numbers
    slots = own_row[...] * deep + rank_row[...].astype(I32) // 2
    own_row[...] = slots

    got_g.wait_recv()
    got_x.wait_recv()

    n = (nx, ny)
    chunk = rows // nx
    tile = rows // (nx * ny)
    here = (x, y)

    def compute(h, rel):
        dest = lax.rem(here[h] + rel, n[h])
        cols = pl.ds(pl.multiple_of(c * half + h * quarter, quarter), quarter)
        for t in range(chunk // tile):
            if h == 0:
                at = dest * chunk + t * tile
            else:
                at = t * (rows // nx) + dest * tile
            at = pl.ds(pl.multiple_of(at, LANES), tile)
            prod[h, rel, t * tile : (t + 1) * tile, :] = dot_t(x_ref[:, at], g_ref[:, cols]) + dot_t(
                xp[:, at], gp[:, h * quarter : (h + 1) * quarter]
            )

    def ring_far(part, buf, up, down, size):
        a, b = (0, size // 2), (size // 2, size // 2)
        return send(part(2, *a), buf.at[0], up), send(part(2, *b), buf.at[1], down)

    def ring_near(part, buf, up, down, size):
        a, b = (0, size // 2), (size // 2, size // 2)
        return send(part(1, *b), buf.at[2], up), send(part(3, *a), buf.at[3], down)

    def ring_join(part, buf, up, down, size, far):
        a, b = (0, size // 2), (size // 2, size // 2)
        far[0].wait_recv()
        ref = part(1, *a)
        ref[...] = ref[...] + buf[0]
        one = send(ref, buf.at[4], up)
        far[1].wait_recv()
        ref = part(3, *b)
        ref[...] = ref[...] + buf[1]
        return one, send(ref, buf.at[5], down)

    def ring_end(part, buf, size, near, join):
        a, b = (0, size // 2), (size // 2, size // 2)
        for copy in near + join:
            copy.wait_recv()
        ref = part(0, *a)
        ref[...] = ref[...] + buf[3] + buf[4]
        ref = part(0, *b)
        ref[...] = ref[...] + buf[2] + buf[5]

    def part1(h):
        return lambda rel, start, size: prod.at[h, rel, pl.ds(start, size)]

    def part2(h):
        def part(rel, start, size):
            dest = lax.rem(here[1 - h] + rel, n[1 - h])
            return prod.at[h, 0, pl.ds(pl.multiple_of(dest * tile + start, 8), size)]

        return part

    ends = ((at_x(1), at_x(nx - 1)), (at_y(1), at_y(ny - 1)))
    second = (ends[1], ends[0])
    far, near, join, far2, near2, join2 = [], [], [], [], [], []
    for h in range(2):
        compute(h, 2)
        far.append(ring_far(part1(h), recv1.at[h], *ends[h], chunk))
    for h in range(2):
        compute(h, 1)
        compute(h, 3)
        near.append(ring_near(part1(h), recv1.at[h], *ends[h], chunk))

    def hop(src, dst, send_sem, recv_sem, device):
        return pltpu.make_async_remote_copy(
            src_ref=src, dst_ref=dst, send_sem=send_sem, recv_sem=recv_sem,
            device_id=device, device_id_type=MESH,
        )

    def ids_one(p):
        at = pl.ds(pl.multiple_of(p * n_dp, 8), n_dp)
        return hop(idsend.at[at], idmid.at[p], t1.at[p], q1.at[p], (dp, at_mp(p)))

    def cold_one(p):
        return hop(send_buf.at[p], mid.at[p], s1.at[p], r1.at[p], (dp, at_mp(p)))

    def ids_two(i):
        to = at_dp(i)
        return hop(idout.at[to], idfin.at[i], t2.at[i], q2.at[i], (to, mp))

    groups = 4
    each = n_mp // groups

    def cold_two(g, i):
        to = at_dp(i)
        at = pl.ds(g * each, each)
        return hop(mid.at[at, to], fin.at[i, at], s2.at[g, i], r2.at[g, i], (to, mp))

    def every_mp(act):
        def body(p, _):
            @pl.when(p != here_slot)
            def _():
                act(p)

            return 0

        lax.fori_loop(0, n_mp, body, 0)

    def every_dp(act):
        def body(i, _):
            act(i)
            return 0

        lax.fori_loop(1, n_dp, body, 0)

    every_mp(lambda p: ids_one(p).start())

    def bucket(p, _):
        for f in range(features):
            lhs[:, f * samples : (f + 1) * samples] = onehot(
                n_dp * deep, own_row[f : f + 1, :] - p * (n_dp * deep)
            )
        block = dot(lhs[...], rhs[...]).astype(BF16)
        send_buf[p] = block.reshape(n_dp, deep, 2 * LANES)

        @pl.when(p != here_slot)
        def _():
            cold_one(p).start()

        return 0

    lax.fori_loop(0, n_mp, bucket, 0)
    mid[here_slot] = send_buf[here_slot]
    idmid[here_slot] = idsend[here_slot * n_dp : (here_slot + 1) * n_dp, :]

    for h in range(2):
        compute(h, 0)
    for h in range(2):
        join.append(ring_join(part1(h), recv1.at[h], *ends[h], chunk, far[h]))

    hot_rows = hp.shape[0]
    hot_ids = hid_ref[...]
    hot_row = jnp.transpose(hot_ids.astype(F32)).astype(I32)
    hot_row = jnp.where(hot_row >= hot_rows, hot_row - hot_rows, hot_row)
    own_row[...] = hot_row
    for f in range(features):
        upper = jnp.broadcast_to(hot_ids[:, f : f + 1], (samples, LANES)) >= hot_rows
        split_columns(rhs, f * samples, pg_ref[:, f * LANES : (f + 1) * LANES], upper)

    def hot_block(m, _):
        for f in range(features):
            lhs[:, f * samples : (f + 1) * samples] = onehot(samples, own_row[f : f + 1, :] - m * samples)
        hpart[pl.ds(pl.multiple_of(m * samples, 8), samples), :] = dot(lhs[...], rhs[...])
        return 0

    lax.fori_loop(0, hot_rows // samples, hot_block, 0)
    got_h = send(hpart.at[:, pl.ds(pl.multiple_of((1 - c) * LANES, LANES), LANES)], hp, partner)
    mine = pl.ds(pl.multiple_of(c * LANES, LANES), LANES)

    every_mp(lambda p: ids_one(p).wait_recv())
    for d in range(n_dp):
        idout[d] = jnp.concatenate([idmid[p, d : d + 1, :] for p in range(n_mp)], axis=0)
    every_dp(lambda i: ids_two(i).start())

    def forward(g):
        for p in range(g * each, (g + 1) * each):
            if p != here_slot:
                cold_one(p).wait_recv()
        every_dp(lambda i: cold_two(g, i).start())
        fin[0, g * each : (g + 1) * each] = mid[g * each : (g + 1) * each, dp]

    forward(0)

    hrx, hry, hrz = hot_rows // nx, hot_rows // (nx * ny), hot_rows // (nx * ny * nz)
    base_x = pl.multiple_of(x * hrx, 8)
    base_y = pl.multiple_of(base_x + y * hry, 8)
    base_z = pl.multiple_of(base_y + z * hrz, 8)
    base_c = pl.multiple_of(c * hot_rows, 8)
    own_z = pl.multiple_of(base_c + base_z, 8)
    got_h.wait_recv()
    hp[...] = hp[...] + hpart[:, mine]
    hots = [
        send(hp.at[pl.ds(pl.multiple_of(lax.rem(x + j, nx) * hrx, 8), hrx)], hx.at[j - 1], at_x(j))
        for j in range(1, nx)
    ]

    every_dp(lambda i: ids_two(i).wait_recv())
    idfin[0] = idout[dp]
    for g in range(groups):
        for i in range(n_dp):
            at = (g * n_dp + i) * each
            idrow[at : at + each, :] = idfin[i, g * each : (g + 1) * each, :]
    digits = idrow[...].astype(BF16)
    at_lane, at_digit = iota((LANES, 2 * LANES), 1), iota((LANES, 2 * LANES), 0)
    want = (at_lane // LANES) * deep + at_lane % deep
    high = dot(digits, jnp.where(at_digit == want, 1.0, 0.0).astype(BF16))
    low = dot(digits, jnp.where(at_digit == want + cap, 1.0, 0.0).astype(BF16))
    numbers = high * 64.0 + low - 64.0
    band8 = LANES // deep
    keep = (iota(numbers.shape, 1) % LANES) // deep == iota(numbers.shape, 0) % band8
    numbers = jnp.where(keep, numbers, 0.0)
    numbers = jnp.sum(numbers.reshape(devices // band8, band8, 2 * LANES), axis=1)
    ids[...] = numbers.astype(I32)

    forward(1)
    for copy in hots:
        copy.wait_recv()
    ref = hp.at[pl.ds(base_x, hrx)]
    ref[...] = ref[...] + hx[0] + hx[1] + hx[2]
    hots = [
        send(hp.at[pl.ds(pl.multiple_of(base_x + lax.rem(y + j, ny) * hry, 8), hry)], hy.at[j - 1], at_y(j))
        for j in range(1, ny)
    ]

    for h in range(2):
        ring_end(part1(h), recv1.at[h], chunk, near[h], join[h])
        far2.append(ring_far(part2(h), recv2.at[h], *second[h], tile))
        near2.append(ring_near(part2(h), recv2.at[h], *second[h], tile))

    for copy in hots:
        copy.wait_recv()
    ref = hp.at[pl.ds(base_y, hry)]
    ref[...] = ref[...] + hy[0] + hy[1] + hy[2]
    hots = [
        send(hp.at[pl.ds(pl.multiple_of(base_y + lax.rem(z + j, nz) * hrz, 8), hrz)], hz.at[j - 1], at_z(j))
        for j in range(1, nz)
    ]

    forward(2)

    cold_half = cold.shape[0]
    per = n_dp * each * deep
    pieces = per // LANES
    eye = iota((LANES, LANES), 0) == iota((LANES, LANES), 1)
    ones = jnp.ones((LANES, LANES), BF16)
    step = 256

    def arrived(g):
        every_dp(lambda i: cold_two(g, i).wait_recv())
        pair = LANES // (each * deep)
        for q in range(pieces):
            grads = fin[q * pair : (q + 1) * pair, g * each : (g + 1) * each].reshape(LANES, 2 * LANES)
            for k in range(2):
                number = ids[g * pieces + q : g * pieces + q + 1, k * LANES : (k + 1) * LANES]
                upper = jnp.where(number >= cold_half, 1.0, 0.0)
                column = dot(jnp.where(eye, upper, 0.0).astype(BF16), ones)
                split_columns(arhs, k * per + q * LANES, grads[:, k * LANES : (k + 1) * LANES], column > 0.5)

    def summed(g, m):
        for q in range(pieces):
            for k in range(2):
                number = ids[g * pieces + q : g * pieces + q + 1, k * LANES : (k + 1) * LANES]
                number = jnp.where(number >= cold_half, number - cold_half, number)
                at = k * per + q * LANES
                alhs[:, at : at + LANES] = onehot(step, number - m * step)
        return dot(alhs[...], arhs[...])

    def gather(g):
        arrived(g)

        def block(m, _):
            at = pl.ds(pl.multiple_of(m * step, 8), step)
            if g == 0:
                cold[at, :] = summed(g, m)
            else:
                cold[at, :] = cold[at, :] + summed(g, m)
            return 0

        lax.fori_loop(0, cold_half // step, block, 0)

    gather(0)

    for copy in hots:
        copy.wait_recv()
    got = hp[pl.ds(base_z, hrz), :]
    for j in range(1, nz):
        got = got + hz[j - 1]
    hsum[pl.ds(own_z, hrz), :] = got
    own = hsum.at[pl.ds(own_z, hrz)]
    hots = [send(own, own, at_z(j)) for j in range(1, nz)]

    for h in range(2):
        join2.append(ring_join(part2(h), recv2.at[h], *second[h], tile, far2[h]))
    forward(3)

    for copy in hots:
        copy.wait_recv()
    own = hsum.at[pl.ds(pl.multiple_of(base_c + base_y, 8), hry)]
    hots = [send(own, own, at_y(j)) for j in range(1, ny)]

    for h in range(2):
        ring_end(part2(h), recv2.at[h], tile, near2[h], join2[h])
        at = pl.multiple_of(here[1 - h] * tile, 8)
        sums[:, h * quarter : (h + 1) * quarter] = prod[h, 0, pl.ds(at, tile), :]
    band = tile // nz
    gots = [
        send(sums.at[pl.ds(pl.multiple_of(lax.rem(z + j, nz) * band, 8), band)], recv3.at[j - 1], at_z(j))
        for j in range(1, nz)
    ]

    gather(1)

    for copy in hots:
        copy.wait_recv()
    own = hsum.at[pl.ds(pl.multiple_of(base_c + base_x, 8), hrx)]
    hots = [send(own, own, at_x(j)) for j in range(1, nx)]

    gather(2)

    for copy in hots:
        copy.wait_recv()
    own = hsum.at[pl.ds(base_c, hot_rows)]
    got_hot = send(own, own, partner)

    value = sums[pl.ds(pl.multiple_of(z * band, 8), band), :]
    for j in range(1, nz):
        gots[j - 1].wait_recv()
        value = value + recv3[j - 1]
    total[...] = value
    out_rows = band // 2
    got = send(total.at[pl.ds(pl.multiple_of((1 - c) * out_rows, 8), out_rows)], last, partner)

    got_hot.wait_recv()
    for i in range(hsum.shape[0] // LANES):
        at = slice(i * LANES, (i + 1) * LANES)
        table, accum = adagrad_block(ht_ref[at, :], ha_ref[i : i + 1, :], hsum[at, :])
        nh_ref[at, :] = table
        nha_ref[i : i + 1, :] = accum

    got.wait_recv()
    own = total[pl.ds(pl.multiple_of(c * out_rows, 8), out_rows), :]
    other = last[...]
    for side in range(2):
        cols = slice(side * half, (side + 1) * half)
        grad = jnp.where(c == side, own, other) * factor
        accum = a_ref[:, cols] + grad * grad
        na_ref[:, cols] = accum
        nw_ref[:, cols] = w_ref[:, cols] - RATE * grad / jnp.sqrt(accum)

    g_last = groups - 1
    arrived(g_last)

    def finish(m, _):
        grads = summed(g_last, m) + cold[pl.ds(pl.multiple_of(m * step, 8), step), :]
        for upper in range(2):
            for part in range(step // LANES):
                row = pl.multiple_of(upper * cold_half + m * step + part * LANES, LANES)
                line = upper * (cold_half // LANES) + m * (step // LANES) + part
                grad = grads[part * LANES : (part + 1) * LANES, upper * LANES : (upper + 1) * LANES]
                table, accum = adagrad_block(
                    ct_ref[pl.ds(row, LANES), :], ca_ref[pl.ds(line, 1), :], grad
                )
                nc_ref[pl.ds(row, LANES), :] = table
                nca_ref[pl.ds(line, 1), :] = accum
        return 0

    lax.fori_loop(0, cold_half // step, finish, 0)

    for copy in copies:
        copy.wait_send()
    every_mp(lambda p: ids_one(p).wait_send())
    every_mp(lambda p: cold_one(p).wait_send())
    every_dp(lambda i: ids_two(i).wait_send())
    for g in range(groups):
        every_dp(lambda i: cold_two(g, i).wait_send())


def shards(
    nx, ny, nz,
    pooled_in, out_grad, pooled_grad, hot_ids, cold_owner, cold_rows,
    mlp_weight, mlp_accum, hot_table, hot_accum, cold_table, cold_accum,
):
    n_dp, n_mp = nx * ny, nz * 2
    devices = n_dp * n_mp
    samples, features = hot_ids.shape
    hid = pooled_in.shape[1]
    hot = hot_table.shape[0]
    rows = cold_table.shape[0]
    lookups = samples * features
    cap = 2 * lookups // devices
    deep = cap // 2
    group_slots = 2 * (n_dp * (n_mp // 4) * deep)
    quarter = hid // 4
    chunk, tile = hid // nx, hid // (nx * ny)
    band = tile // nz
    half_hot = hot // 2
    hrx, hry, hrz = half_hot // nx, half_hot // (nx * ny), half_hot // (nx * ny * nz)
    n_copies = 3 + 2 * 6 * 2 + (nz - 1) + 1 + 2 * (nx - 1 + ny - 1 + nz - 1) + 1
    dma = pltpu.SemaphoreType.DMA
    outs = pl.pallas_call(
        functools.partial(step_kernel, nx, ny, nz, cap, float(samples * devices) ** (-0.5)),
        out_shape=(
            jax.ShapeDtypeStruct(mlp_weight.shape, F32),
            jax.ShapeDtypeStruct(mlp_accum.shape, F32),
            jax.ShapeDtypeStruct(hot_table.shape, F32),
            jax.ShapeDtypeStruct((hot // LANES, LANES), F32),
            jax.ShapeDtypeStruct(cold_table.shape, F32),
            jax.ShapeDtypeStruct((rows // LANES, LANES), F32),
        ),
        in_specs=[VMEM] * 12,
        out_specs=(VMEM,) * 6,
        scratch_shapes=[
            pltpu.VMEM((samples, hid), BF16),
            pltpu.VMEM((samples, hid // 2), BF16),
            pltpu.VMEM((2, 4, chunk, quarter), F32),
            pltpu.VMEM((2, 6, chunk // 2, quarter), F32),
            pltpu.VMEM((2, 6, tile // 2, quarter), F32),
            pltpu.VMEM((tile, hid // 2), F32),
            pltpu.VMEM((nz - 1, band, hid // 2), F32),
            pltpu.VMEM((band, hid // 2), F32),
            pltpu.VMEM((band // 2, hid // 2), F32),
            pltpu.VMEM((half_hot, 2 * LANES), F32),
            pltpu.VMEM((half_hot, LANES), F32),
            pltpu.VMEM((nx - 1, hrx, LANES), F32),
            pltpu.VMEM((ny - 1, hry, LANES), F32),
            pltpu.VMEM((nz - 1, hrz, LANES), F32),
            pltpu.VMEM((hot, LANES), F32),
            pltpu.VMEM((features, samples), F32),
            pltpu.VMEM((features, samples), I32),
            pltpu.VMEM((lookups, 2 * LANES), BF16),
            pltpu.VMEM((samples, lookups), BF16),
            pltpu.VMEM((n_mp, n_dp, deep, 2 * LANES), BF16),
            pltpu.VMEM((n_mp, n_dp, deep, 2 * LANES), BF16),
            pltpu.VMEM((n_dp, n_mp, deep, 2 * LANES), BF16),
            pltpu.VMEM((devices, LANES), F32),
            pltpu.VMEM((n_mp, n_dp, LANES), F32),
            pltpu.VMEM((n_dp, n_mp, LANES), F32),
            pltpu.VMEM((n_dp, n_mp, LANES), F32),
            pltpu.VMEM((devices, LANES), F32),
            pltpu.VMEM((devices * deep // LANES, 2 * LANES), I32),
            pltpu.VMEM((group_slots, 2 * LANES), BF16),
            pltpu.VMEM((256, group_slots), BF16),
            pltpu.VMEM((rows // 2, 2 * LANES), F32),
            dma((n_copies,)), dma((n_copies,)),
            dma((n_mp,)), dma((n_mp,)),
            dma((4, n_dp)), dma((4, n_dp)),
            dma((n_mp,)), dma((n_mp,)),
            dma((n_dp,)), dma((n_dp,)),
        ],
        compiler_params=pltpu.CompilerParams(
            vmem_limit_bytes=58 << 20, collective_id=0, has_side_effects=True
        ),
        name="step",
    )(
        pooled_in, out_grad, pooled_grad, hot_ids, cold_owner.T, cold_rows, mlp_weight, mlp_accum,
        hot_table, hot_accum.reshape(hot // LANES, LANES),
        cold_table, cold_accum.reshape(rows // LANES, LANES),
    )
    new_weight, new_mlp_accum, new_hot, new_hot_accum, new_cold, new_cold_accum = outs
    return (
        new_weight,
        new_mlp_accum,
        new_hot,
        new_hot_accum.reshape(hot),
        new_cold,
        new_cold_accum.reshape(rows),
    )


def solution(mesh):
    split = P(("dp", "mp"), None)
    nx = ny = 4
    nz = mesh.shape["mp"] // 2
    return jax.shard_map(
        functools.partial(shards, nx, ny, nz),
        mesh=mesh,
        in_specs=(split,) * 8 + (P(), P(), split, P(("dp", "mp"))),
        out_specs=(split, split, P(), P(), split, P(("dp", "mp"))),
        check_vma=False,
    )
```

time: 190 us -> 132 us (0.69)
  blocking collectives: 29.1 us -> 0 us
  Pallas kernels: 141 us -> 120 us
  starting transfers between devices: 7.35 us -> 0 us
  other arithmetic: 2.37 us -> 0 us
  local copies, waits for them, and re-layouts: 8.66 us -> 10.8 us
    all_to_all x1 -> x0, blocking collectives: 29.1 us -> none  [shards(): lax.all_to_all(ids[:, :cap], ('dp', 'mp'), split_axis=0, concat_axis=0, t...]
    pallas_call x4 -> x1, Pallas kernels: 141 us -> 120 us  [shards(): pl.pallas_call(functools.partial(step_kernel, nx, ny, nz, cap, float(samp...]
    all_to_all x1 -> x0, starting transfers between devices: 7.35 us -> none  [shards(): lax.all_to_all(send_grad.reshape(devices, cap // 2, 2 * LANES), ('dp', 'm...]
    unnamed x29 -> x14, local copies, waits for them, and re-layouts: 6.76 us -> 10.8 us
    reshape x4 -> x0, local copies, waits for them, and re-layouts: 1.9 us -> none  [the longest x2 1.75 us: shards(): id_col = got_ids.reshape(slots, 2)]
  transfers between devices with their start and end apart: 1 -> 0, of which waited for: 0 -> 0; matrix products, arithmetic and copies ran while one was open for 1% -> 0% of each run, Pallas kernels for 57% -> 0%
where the time goes in v2:
time: 132 us
  Pallas kernels  120 us (91%)
  local copies, waits for them, and re-layouts  10.8 us (8%)
    pallas_call x1, Pallas kernels, shards(): pl.pallas_call(functools.partial(step_kernel, nx, ny, nz, cap, float(samp...  120 us
    unnamed x14, local copies, waits for them, and re-layouts  10.8 us

profile of v2, /device:TPU:1, one launch (start us, length us, event | category | flops | bytes accessed | tf_op | source)
XLA Modules:
  0.0 131.5 jit_solution(10431103803959159039)
XLA Ops:
  0.6 1.5 %copy.18.hid_ref = s32[256,16]{1,0:T(8,128)} copy(s32[256,16]{0,1:T(8,128)} %param.15) | data formatting | bytes 32768 | tf_op args[3]
  2.1 1.5 %copy.19.row_ref = s32[256,16]{1,0:T(8,128)} copy(s32[256,16]{0,1:T(8,128)} %param.17) | data formatting | bytes 32768 | tf_op args[5]
  3.6 120.0 %step.1 = (f32[8,2048]{1,0:T(8,128)}, f32[8,2048]{1,0:T(8,128)}, f32[2048,128]{1,0:T(8,128)}, f32[16,128]{1,0:T(8,128)}, f32[4096,128]{1,0:T(8,128)}, /*index=5*/f32[32,128]{1,0:T(8,128)}) custom-call(bf16[256,2048]{1,0:T(8,128)(2,1)} %x_ref.1, bf16[256,2048]{1,0:T(8,128)(2,1)} %g_ref.1, bf16[256,2048]{1,0:T(8,128)(2,1)} %pg_ref.1, s32[256,16]{1,0:T(8,128)} %copy.18.hid_ref, ...), custom_call_target="tpu_custom_call" | custom-call | tf_op jit(solution)/shard_map/step/pallas_call | solution.py:558
  123.6 0.0 copy-start.2
  123.6 0.0 copy-start
  123.7 1.6 %copy.26 = f32[8,2048]{1,0:T(8,128)} copy(f32[8,2048]{1,0:T(8,128)} %get-tuple-element.24) | data formatting | bytes 131072
  125.3 1.5 %copy.27 = f32[8,2048]{1,0:T(8,128)} copy(f32[8,2048]{1,0:T(8,128)} %get-tuple-element.25) | data formatting | bytes 131072
  126.7 2.3 %copy.28 = f32[2048,128]{1,0:T(8,128)} copy(f32[2048,128]{1,0:T(8,128)} %get-tuple-element.26) | data formatting | bytes 2097152
  129.0 0.0 copy-done.2
  129.0 0.6 copy.29
  129.6 0.0 copy-done
  129.6 0.0 copy-start.1
  129.6 1.3 %copy.30 = f32[4096,128]{1,0:T(8,128)} copy(f32[4096,128]{1,0:T(8,128)S(1)} %copy-done) | data formatting | bytes 4194304
  130.9 0.0 copy-done.1
  130.9 0.6 copy.31
Async XLA Ops:
  123.6 5.4 %copy-start.2 = (f32[16,128]{1,0:T(8,128)S(1)}, f32[16,128]{1,0:T(8,128)}, u32[]{:S(2)}) copy-start(f32[16,128]{1,0:T(8,128)} %get-tuple-element.15) | copy-start | bytes 24580
  123.6 6.0 %copy-start = (f32[4096,128]{1,0:T(8,128)S(1)}, f32[4096,128]{1,0:T(8,128)}, u32[]{:S(2)}) copy-start(f32[4096,128]{1,0:T(8,128)} %get-tuple-element.28) | copy-start | bytes 6291460
  129.6 1.3 %copy-start.1 = (f32[32,128]{1,0:T(8,128)S(1)}, f32[32,128]{1,0:T(8,128)}, u32[]{:S(2)}) copy-start(f32[32,128]{1,0:T(8,128)} %get-tuple-element.17) | copy-start | bytes 49156

commit v3 on v2

v3 whole, which is shorter than its diff:
```python
import functools

import jax
import jax.numpy as jnp
from jax import lax
from jax.experimental import pallas as pl
from jax.experimental.pallas import tpu as pltpu
from jax.sharding import PartitionSpec as P

MESH = pl.DeviceIdType.MESH
RATE = 0.1
LANES = 128
F32 = jnp.float32
BF16 = jnp.bfloat16
I32 = jnp.int32
VMEM = pl.BlockSpec(memory_space=pltpu.VMEM)


SPLITS = 2
STEPS = 2

PLAN = (
    ("cores",), ("far", 0), ("far", 1), ("near", 0), ("near", 1), ("bucket", 0),
    ("far", 2), ("far", 3), ("near", 2), ("near", 3), ("bucket", 1), ("bucket", 2),
    ("own", 0), ("own", 1), ("own", 2), ("own", 3), ("join", 0), ("join", 1), ("bucket", 3), ("join", 2), ("join", 3),
    ("numbers_on",), ("hot_product",), ("forward", 0), ("numbers_in",), ("hot_scatter", "x"), ("forward", 1),
    ("hot_scatter", "y"), ("end", 0), ("end", 1), ("hot_scatter", "z"), ("end", 2), ("end", 3), ("gather", 0),
    ("join2", 0), ("join2", 1), ("join2", 2), ("join2", 3), ("forward", 2), ("hot_gather", "z"),
    ("end2", 0), ("end2", 1), ("along_z", 0), ("end2", 2), ("end2", 3), ("along_z", 1), ("gather", 1),
    ("hot_gather", "y"), ("forward", 3), ("end_z", 0), ("end_z", 1), ("hot_gather", "x"), ("gather", 2),
    ("weights", 0), ("weights", 1), ("hot_gather", "core"), ("gather", 3), ("hot_wait",),
)


def iota(shape, axis):
    return lax.broadcasted_iota(I32, shape, axis)


def onehot(rows, values):
    number = iota((rows, values.shape[1]), 0).astype(F32).astype(BF16)
    match = number == jnp.broadcast_to(values.astype(F32).astype(BF16), number.shape)
    return jnp.where(match, jnp.ones_like(number), jnp.zeros_like(number))


def lookup(values, table):
    out = jnp.zeros_like(values)
    for at, entry in enumerate(table):
        out = jnp.where(values == at, entry, out)
    return out


def dot(a, b):
    return lax.dot_general(a, b, (((1,), (0,)), ((), ())), preferred_element_type=F32)


def dot_t(a, b):
    return lax.dot_general(a, b, (((0,), (0,)), ((), ())), preferred_element_type=F32)


def adagrad_block(table, accum_row, grad):
    eye = iota((LANES, LANES), 0) == iota((LANES, LANES), 1)
    accum = jnp.sum(jnp.where(eye, accum_row, 0.0), axis=1, keepdims=True)
    new_accum = accum + jnp.sum(grad * grad, axis=1, keepdims=True) * (1.0 / LANES)
    new_table = table - grad * (RATE / jnp.sqrt(new_accum))
    new_row = jnp.sum(jnp.where(eye, new_accum, 0.0), axis=0, keepdims=True)
    return new_table, new_row


def dot_nt(a, b):
    return lax.dot_general(a, b, (((1,), (1,)), ((), ())), preferred_element_type=F32)


def split_columns(rhs, at, grad, upper):
    zero = jnp.zeros_like(grad)
    rows = grad.shape[0]
    rhs[at : at + rows, :LANES] = jnp.where(upper, zero, grad)
    rhs[at : at + rows, LANES:] = jnp.where(upper, grad, zero)


def step_kernel(
    nx, ny, nz, splits, cap, factor,
    x_ref, g_ref, pg_ref, hid_ref, own_ref, row_ref,
    wg_ref, hsum, cold,
    xp, gp, prod, recv1, recv2, sums, recv3, total, last,
    hot_rhs, hot_at, hpart, hp, hx, hy, hz,
    rank_row, own_row, rhs, lhs, send_buf, mid, fin, idsend, idmid, idout, idfin, ids, arhs, alhs,
    ss, rs, s1, r1, s2, r2, t1, q1, t2, q2,
):
    features, samples = hid_ref.shape
    n_dp, n_mp = nx * ny, nz * 2
    devices = n_dp * n_mp
    deep = cap // 2
    dp, mp = lax.axis_index("dp"), lax.axis_index("mp")
    x, y = lax.div(dp, ny), lax.rem(dp, ny)
    z, c = lax.div(mp, 2), lax.rem(mp, 2)

    def at_x(j):
        return (lax.rem(x + j, nx) * ny + y, mp)

    def at_y(j):
        return (x * ny + lax.rem(y + j, ny), mp)

    def at_z(j):
        return (dp, lax.rem(z + j, nz) * 2 + c)

    far_first = ((1, 2), (3, 2), (2, 1), (2, 3), (1, 1), (3, 3), (2, 0), (0, 2))
    far_first += ((1, 3), (3, 1), (2, 2), (0, 0), (1, 0), (3, 0), (0, 1), (0, 3))
    here_dp = far_first.index((0, 0))
    dp_slot = [far_first.index((i // ny, i % ny)) for i in range(n_dp)]

    def at_dp(i):
        dx, dy = far_first[i]
        return (lax.rem(x + dx, nx) * ny + lax.rem(y + dy, ny), mp)

    mid_z = nz // 2

    def at_mp(p):
        pz, pc = lax.div(p, 2), lax.rem(p, 2)
        jz = jnp.where(lax.rem(pz, 2) == 1, mid_z - lax.div(pz + 1, 2), mid_z + lax.div(pz, 2))
        return lax.rem(z + jz, nz) * 2 + lax.rem(c + pc, 2)

    here_slot = n_mp - 2
    partner = (dp, z * 2 + 1 - c)
    barrier = pltpu.get_barrier_semaphore()

    def greet_dp(i, _):
        pl.semaphore_signal(barrier, inc=1, device_id=(lax.rem(dp + i, n_dp), mp), device_id_type=MESH)
        return 0

    def greet_mp(j, _):
        pl.semaphore_signal(
            barrier, inc=1, device_id=(dp, lax.rem(mp + j, n_mp)), device_id_type=MESH
        )
        return 0

    lax.fori_loop(1, n_dp, greet_dp, 0)
    lax.fori_loop(1, n_mp, greet_mp, 0)

    line = LANES // features
    spread = jnp.concatenate(
        [
            jnp.broadcast_to(own_ref[:, r * LANES : (r + 1) * LANES], (line, LANES))
            for r in range(own_ref.shape[1] // LANES)
        ],
        axis=0,
    )
    keep = iota((samples, LANES), 1) // features == iota((samples, LANES), 0) % line
    pick = jnp.where(iota((features, LANES), 1) % features == iota((features, LANES), 0), 1.0, 0.0)
    owner = dot_nt(pick.astype(BF16), jnp.where(keep, spread, 0).astype(F32).astype(BF16)).astype(I32)
    to_mp = owner % n_mp
    jz = (to_mp // 2 - z + nz) % nz
    pz = jnp.where(jz > mid_z, 2 * (jz - mid_z), jnp.maximum(2 * (mid_z - jz) - 1, 0))
    to_mp = pz * 2 + (to_mp + c) % 2
    to_dp = owner // n_mp
    to_dp = lookup((to_dp // ny - x + nx) % nx * ny + (to_dp % ny - y + ny) % ny, dp_slot)
    quarters = 4
    each = n_dp // quarters
    own_row[...] = (to_dp // each * n_mp + to_mp) * each + to_dp % each
    id_place = to_mp * n_dp + to_dp
    earlier = jnp.where(
        iota((samples, samples), 0) < iota((samples, samples), 1), 1.0, 0.0
    ).astype(BF16)
    base = jnp.zeros((devices, 1), F32)
    for f in range(features):
        hot = onehot(devices, own_row[f : f + 1, :])
        hot32 = hot.astype(F32)
        before = dot(hot, earlier) + base
        rank_row[f : f + 1, :] = jnp.sum(hot32 * before, axis=0, keepdims=True)
        base = base + jnp.sum(hot32, axis=1, keepdims=True)

    rank_col = jnp.transpose(rank_row[...]).astype(I32)
    for f in range(features):
        odd = jnp.broadcast_to(rank_col[:, f : f + 1], (samples, LANES)) % 2 == 1
        split_columns(rhs, f * samples, pg_ref[:, f * LANES : (f + 1) * LANES], odd)
    slots = own_row[...] * deep + rank_row[...].astype(I32) // 2
    own_row[...] = slots

    pl.semaphore_wait(barrier, n_dp + n_mp - 2)

    copies = []

    def send(src, dst, device):
        k = len(copies)
        copy = pltpu.make_async_remote_copy(
            src_ref=src, dst_ref=dst, send_sem=ss.at[k], recv_sem=rs.at[k],
            device_id=device, device_id_type=MESH,
        )
        copy.start()
        copies.append(copy)
        return copy

    half = g_ref.shape[1] // 2
    quarter = half // 2
    rows = x_ref.shape[1]
    got_g = send(g_ref.at[:, pl.ds(pl.multiple_of((1 - c) * half, half), half)], gp, partner)
    got_x = send(x_ref, xp, partner)

    lane = iota((samples, LANES), 1)
    row_col = jnp.transpose(row_ref[...].astype(F32)).astype(I32)
    numbers = jnp.zeros((devices, LANES), F32)
    for f in range(features):
        rank = jnp.broadcast_to(rank_col[:, f : f + 1], (samples, LANES))
        row = jnp.broadcast_to(row_col[:, f : f + 1], (samples, LANES))
        spot = (rank % 2) * deep + rank // 2
        digit = jnp.where(lane < cap, row // 64 + 1, row % 64)
        digit = jnp.where((lane % cap == spot) & (lane < 2 * cap), digit, 0).astype(F32).astype(BF16)
        numbers += dot(onehot(devices, id_place[f : f + 1, :]), digit)
    idsend[...] = numbers

    def hop(src, dst, send_sem, recv_sem, device):
        return pltpu.make_async_remote_copy(
            src_ref=src, dst_ref=dst, send_sem=send_sem, recv_sem=recv_sem,
            device_id=device, device_id_type=MESH,
        )

    def ids_one(p):
        at = pl.ds(pl.multiple_of(p * n_dp, 8), n_dp)
        return hop(idsend.at[at], idmid.at[p], t1.at[p], q1.at[p], (dp, at_mp(p)))

    def cold_one(q, p):
        return hop(send_buf.at[q, p], mid.at[q, p], s1.at[q, p], r1.at[q, p], (dp, at_mp(p)))

    def ids_two(i):
        return hop(idout.at[i], idfin.at[i], t2.at[i], q2.at[i], at_dp(i))

    def cold_two(q, k):
        return hop(mid.at[q, :, k], fin.at[q, k], s2.at[q, k], r2.at[q, k], at_dp(q * each + k))

    def every_mp(act):
        def body(p, _):
            @pl.when(p != here_slot)
            def _():
                act(p)

            return 0

        lax.fori_loop(0, n_mp, body, 0)

    others = [i for i in range(n_dp) if i != here_dp]
    every_mp(lambda p: ids_one(p).start())
    blocks = samples // (each * deep)

    def bucket(m, _):
        for f in range(features):
            lhs[:, f * samples : (f + 1) * samples] = onehot(samples, own_row[f : f + 1, :] - m * samples)
        block = dot(lhs[...], rhs[...]).astype(BF16)
        q, first = lax.div(m * blocks, n_mp), lax.rem(m * blocks, n_mp)
        send_buf[q, pl.ds(first, blocks)] = block.reshape(blocks, each, deep, 2 * LANES)
        for k in range(blocks):
            p = first + k

            @pl.when(p != here_slot)
            def _():
                cold_one(q, p).start()

        return 0

    per_quarter = n_mp // blocks
    n = (nx, ny)
    chunk = rows // nx
    tile = rows // (nx * ny)
    here = (x, y)
    ends = ((at_x(1), at_x(nx - 1)), (at_y(1), at_y(ny - 1)))
    second = (ends[1], ends[0])
    width = quarter // splits
    todo = {}

    def bucket_quarter(q):
        lax.fori_loop(q * per_quarter, (q + 1) * per_quarter, bucket, 0)
        mid[q, here_slot] = send_buf[q, here_slot]

    def cores():
        got_g.wait_recv()
        got_x.wait_recv()

    def compute(u, rel):
        h, k = u % 2, u // 2
        dest = lax.rem(here[h] + rel, n[h])
        first = h * quarter + k * width
        cols = pl.ds(pl.multiple_of(c * half + first, width), width)
        for t in range(chunk // tile):
            if h == 0:
                at = dest * chunk + t * tile
            else:
                at = t * (rows // nx) + dest * tile
            at = pl.ds(pl.multiple_of(at, LANES), tile)
            prod[u, rel, t * tile : (t + 1) * tile, :] = dot_t(x_ref[:, at], g_ref[:, cols]) + dot_t(
                xp[:, at], gp[:, first : first + width]
            )

    def cut(rel, size, second_half):
        return (rel, size // 2 if second_half else 0, size // 2)

    def ring_far(key, part, buf, up, down, size):
        todo[key, "far"] = (
            send(part(*cut(2, size, False)), buf.at[0], up),
            send(part(*cut(2, size, True)), buf.at[1], down),
        )

    def ring_near(key, part, buf, up, down, size):
        todo[key, "near"] = (
            send(part(*cut(1, size, True)), buf.at[2], up),
            send(part(*cut(3, size, False)), buf.at[3], down),
        )

    def ring_join(key, part, buf, up, down, size):
        one, two = todo[key, "far"]
        one.wait_recv()
        ref = part(*cut(1, size, False))
        ref[...] = ref[...] + buf[0]
        one = send(ref, buf.at[4], up)
        two.wait_recv()
        ref = part(*cut(3, size, True))
        ref[...] = ref[...] + buf[1]
        todo[key, "join"] = (one, send(ref, buf.at[5], down))

    def ring_end(key, part, buf, up, down, size):
        for copy in todo[key, "near"] + todo[key, "join"]:
            copy.wait_recv()
        ref = part(*cut(0, size, False))
        ref[...] = ref[...] + buf[3] + buf[4]
        ref = part(*cut(0, size, True))
        ref[...] = ref[...] + buf[2] + buf[5]

    def part1(u):
        return lambda rel, start, size: prod.at[u, rel, pl.ds(start, size)]

    def part2(u):
        axis = 1 - u % 2

        def part(rel, start, size):
            dest = lax.rem(here[axis] + rel, n[axis])
            return prod.at[u, 0, pl.ds(pl.multiple_of(dest * tile + start, 8), size)]

        return part

    def one(u):
        return ((1, u), part1(u), recv1.at[u], *ends[u % 2], chunk)

    def two(u):
        return ((2, u), part2(u), recv2.at[u], *second[u % 2], tile)

    def far(u):
        compute(u, 2)
        ring_far(*one(u))

    def near(u):
        compute(u, 1)
        compute(u, 3)
        ring_near(*one(u))

    def own(u):
        compute(u, 0)

    def join(u):
        ring_join(*one(u))

    def end(u):
        ring_end(*one(u))
        ring_far(*two(u))
        ring_near(*two(u))

    def join2(u):
        ring_join(*two(u))

    band = tile // nz

    def end2(u):
        ring_end(*two(u))
        h, k = u % 2, u // 2
        at = pl.multiple_of(here[1 - h] * tile, 8)
        sums[k, :, h * width : (h + 1) * width] = prod[u, 0, pl.ds(at, tile), :]

    def along_z(k):
        todo["z", k] = [
            send(
                sums.at[k, pl.ds(pl.multiple_of(lax.rem(z + j, nz) * band, 8), band)],
                recv3.at[k, j - 1],
                at_z(j),
            )
            for j in range(1, nz)
        ]

    out_rows = band // 2

    def end_z(k):
        value = sums[k, pl.ds(pl.multiple_of(z * band, 8), band), :]
        for j in range(1, nz):
            todo["z", k][j - 1].wait_recv()
            value = value + recv3[k, j - 1]
        total[k] = value
        other_rows = pl.ds(pl.multiple_of((1 - c) * out_rows, 8), out_rows)
        todo["last", k] = send(total.at[k, other_rows], last.at[k], partner)

    def weights(k):
        todo["last", k].wait_recv()
        mine = total[k, pl.ds(pl.multiple_of(c * out_rows, 8), out_rows), :]
        other = last[k]
        for side in range(2):
            grad = jnp.where(c == side, mine, other) * factor
            for h in range(2):
                at = side * half + h * quarter + k * width
                wg_ref[:, at : at + width] = grad[:, h * width : (h + 1) * width]

    def at_first(j):
        return (jnp.where(c == 0, at_x(j)[0], at_y(j)[0]), mp)

    def at_second(j):
        return (jnp.where(c == 0, at_y(j)[0], at_x(j)[0]), mp)

    first, next_one = jnp.where(c == 0, x, y), jnp.where(c == 0, y, x)
    hot_rows = hp.shape[0]
    hrx, hry, hrz = hot_rows // nx, hot_rows // (nx * ny), hot_rows // (nx * ny * nz)
    base_x = pl.multiple_of(first * hrx, 8)
    base_y = pl.multiple_of(base_x + next_one * hry, 8)
    base_z = pl.multiple_of(base_y + z * hrz, 8)
    base_c = pl.multiple_of(c * hot_rows, 8)

    def hot_product():
        hot_row = hid_ref[...]
        hot_ids = jnp.transpose(hot_row.astype(F32)).astype(I32)
        hot_at[...] = jnp.where(hot_row >= hot_rows, hot_row - hot_rows, hot_row)
        for f in range(features):
            upper = jnp.broadcast_to(hot_ids[:, f : f + 1], (samples, LANES)) >= hot_rows
            split_columns(hot_rhs, f * samples, pg_ref[:, f * LANES : (f + 1) * LANES], upper)

        def hot_block(m, _):
            for f in range(features):
                lhs[:, f * samples : (f + 1) * samples] = onehot(samples, hot_at[f : f + 1, :] - m * samples)
            hpart[pl.ds(pl.multiple_of(m * samples, 8), samples), :] = dot(lhs[...], hot_rhs[...])
            return 0

        lax.fori_loop(0, hot_rows // samples, hot_block, 0)
        theirs = hpart.at[:, pl.ds(pl.multiple_of((1 - c) * LANES, LANES), LANES)]
        todo["hot"] = [send(theirs, hp, partner)]

    def hot_wait():
        for copy in todo["hot"]:
            copy.wait_recv()

    def hot_scatter(axis):
        hot_wait()
        if axis == "x":
            hp[...] = hp[...] + hpart[:, pl.ds(pl.multiple_of(c * LANES, LANES), LANES)]
            base, size, buf, me, count, at = 0, hrx, hx, first, nx, at_first
        elif axis == "y":
            ref = hp.at[pl.ds(base_x, hrx)]
            ref[...] = ref[...] + hx[0] + hx[1] + hx[2]
            base, size, buf, me, count, at = base_x, hry, hy, next_one, ny, at_second
        else:
            ref = hp.at[pl.ds(base_y, hry)]
            ref[...] = ref[...] + hy[0] + hy[1] + hy[2]
            base, size, buf, me, count, at = base_y, hrz, hz, z, nz, at_z
        todo["hot"] = [
            send(hp.at[pl.ds(pl.multiple_of(base + lax.rem(me + j, count) * size, 8), size)], buf.at[j - 1], at(j))
            for j in range(1, count)
        ]

    def hot_gather(axis):
        hot_wait()
        if axis == "z":
            got = hp[pl.ds(base_z, hrz), :]
            for j in range(1, nz):
                got = got + hz[j - 1]
            own_z = pl.multiple_of(base_c + base_z, 8)
            hsum[pl.ds(own_z, hrz), :] = got
            ref, peers = hsum.at[pl.ds(own_z, hrz)], [at_z(j) for j in range(1, nz)]
        elif axis == "y":
            ref = hsum.at[pl.ds(pl.multiple_of(base_c + base_y, 8), hry)]
            peers = [at_second(j) for j in range(1, ny)]
        elif axis == "x":
            ref = hsum.at[pl.ds(pl.multiple_of(base_c + base_x, 8), hrx)]
            peers = [at_first(j) for j in range(1, nx)]
        else:
            ref, peers = hsum.at[pl.ds(base_c, hot_rows)], [partner]
        todo["hot"] = [send(ref, ref, peer) for peer in peers]

    def numbers_on():
        every_mp(lambda p: ids_one(p).wait_recv())
        idmid[here_slot] = idsend[here_slot * n_dp : (here_slot + 1) * n_dp, :]
        for i in range(n_dp):
            idout[i] = jnp.concatenate([idmid[p, i : i + 1, :] for p in range(n_mp)], axis=0)
        for i in others:
            ids_two(i).start()

    band8 = LANES // deep

    def numbers_in():
        for i in others:
            ids_two(i).wait_recv()
        idfin[here_dp] = idout[here_dp]
        digits = idfin[...].reshape(devices, LANES).astype(BF16)
        at_lane, at_digit = iota((LANES, 2 * LANES), 1), iota((LANES, 2 * LANES), 0)
        want = (at_lane // LANES) * deep + at_lane % deep
        high = dot(digits, jnp.where(at_digit == want, 1.0, 0.0).astype(BF16))
        low = dot(digits, jnp.where(at_digit == want + cap, 1.0, 0.0).astype(BF16))
        numbers = high * 64.0 + low - 64.0
        keep = (iota(numbers.shape, 1) % LANES) // deep == iota(numbers.shape, 0) % band8
        numbers = jnp.where(keep, numbers, 0.0)
        numbers = jnp.sum(numbers.reshape(devices // band8, band8, 2 * LANES), axis=1)
        ids[...] = numbers.astype(I32)

    def forward(q):
        every_mp(lambda p: cold_one(q, p).wait_recv())
        for k in range(each):
            if q * each + k == here_dp:
                fin[q, k] = mid[q, :, k]
            else:
                cold_two(q, k).start()

    cold_half = cold.shape[0]
    per = each * n_mp * deep
    pieces = per // LANES
    step = 256

    def gather(g):
        for k in range(each):
            if g * each + k != here_dp:
                cold_two(g, k).wait_recv()
        eye = iota((LANES, LANES), 0) == iota((LANES, LANES), 1)
        ones = jnp.ones((LANES, LANES), BF16)
        for q in range(pieces):
            run = q % (n_mp // band8) * band8
            grads = fin[g, q // (n_mp // band8), run : run + band8].reshape(LANES, 2 * LANES)
            for k in range(2):
                number = ids[g * pieces + q : g * pieces + q + 1, k * LANES : (k + 1) * LANES]
                upper = jnp.where(number >= cold_half, 1.0, 0.0)
                column = dot(jnp.where(eye, upper, 0.0).astype(BF16), ones)
                split_columns(arhs, k * per + q * LANES, grads[:, k * LANES : (k + 1) * LANES], column > 0.5)

        def block(m, _):
            for q in range(pieces):
                for k in range(2):
                    number = ids[g * pieces + q : g * pieces + q + 1, k * LANES : (k + 1) * LANES]
                    number = jnp.where(number >= cold_half, number - cold_half, number)
                    at = k * per + q * LANES
                    alhs[:, at : at + LANES] = onehot(step, number - m * step)
            at = pl.ds(pl.multiple_of(m * step, 8), step)
            part = dot(alhs[...], arhs[...])
            if g == 0:
                cold[at, :] = part
            else:
                cold[at, :] = cold[at, :] + part
            return 0

        lax.fori_loop(0, cold_half // step, block, 0)

    for action, *given in PLAN:
        {
            "bucket": bucket_quarter, "cores": cores, "far": far, "near": near, "own": own, "join": join,
            "end": end, "join2": join2, "end2": end2, "along_z": along_z, "end_z": end_z, "weights": weights,
            "hot_product": hot_product, "hot_scatter": hot_scatter, "hot_gather": hot_gather, "hot_wait": hot_wait,
            "numbers_on": numbers_on, "numbers_in": numbers_in, "forward": forward, "gather": gather,
        }[action](*given)

    for copy in copies:
        copy.wait_send()
    every_mp(lambda p: ids_one(p).wait_send())
    for q in range(quarters):
        every_mp(lambda p: cold_one(q, p).wait_send())
    for i in others:
        ids_two(i).wait_send()
        cold_two(i // each, i % each).wait_send()


def update_kernel(
    wg_ref, hot_ref, cold_ref, w_ref, a_ref, ht_ref, ha_ref, ct_ref, ca_ref,
    nw_ref, na_ref, nh_ref, nha_ref, nc_ref, nca_ref,
):
    m, steps = pl.program_id(0), pl.num_programs(0)

    @pl.when(m == 0)
    def _():
        grad = wg_ref[...]
        accum = a_ref[...] + grad * grad
        na_ref[...] = accum
        nw_ref[...] = w_ref[...] - RATE * grad / jnp.sqrt(accum)

    parts = hot_ref.shape[0] // LANES
    for part in range(parts):
        at, line = slice(part * LANES, (part + 1) * LANES), pl.ds(m * parts + part, 1)
        nh_ref[at, :], nha_ref[line, :] = adagrad_block(ht_ref[at, :], ha_ref[line, :], hot_ref[at, :])
    parts = cold_ref.shape[0] // LANES
    for upper in range(2):
        for part in range(parts):
            at, line = slice(part * LANES, (part + 1) * LANES), pl.ds((upper * steps + m) * parts + part, 1)
            grad = cold_ref[at, upper * LANES : (upper + 1) * LANES]
            nc_ref[upper, at, :], nca_ref[line, :] = adagrad_block(ct_ref[upper, at, :], ca_ref[line, :], grad)


def shards(
    nx, ny, nz,
    pooled_in, out_grad, pooled_grad, hot_ids, cold_owner, cold_rows,
    mlp_weight, mlp_accum, hot_table, hot_accum, cold_table, cold_accum,
):
    n_dp, n_mp = nx * ny, nz * 2
    devices = n_dp * n_mp
    samples, features = hot_ids.shape
    hid = pooled_in.shape[1]
    hot = hot_table.shape[0]
    rows = cold_table.shape[0]
    lookups = samples * features
    cap = 2 * lookups // devices
    deep = cap // 2
    group_slots = 2 * (n_dp * (n_mp // 4) * deep)
    quarter = hid // 4
    chunk, tile = hid // nx, hid // (nx * ny)
    band = tile // nz
    half_hot = hot // 2
    hrx, hry, hrz = half_hot // nx, half_hot // (nx * ny), half_hot // (nx * ny * nz)
    pieces = 2 * SPLITS
    width = quarter // SPLITS
    n_copies = 4 + pieces * 6 * 2 + SPLITS * nz + 2 * (nx - 1 + ny - 1 + nz - 1)
    dma = pltpu.SemaphoreType.DMA
    weight_grad, hot_grad, cold_grad = pl.pallas_call(
        functools.partial(step_kernel, nx, ny, nz, SPLITS, cap, float(samples * devices) ** (-0.5)),
        out_shape=(
            jax.ShapeDtypeStruct(mlp_weight.shape, F32),
            jax.ShapeDtypeStruct(hot_table.shape, F32),
            jax.ShapeDtypeStruct((rows // 2, 2 * LANES), F32),
        ),
        in_specs=[VMEM] * 6,
        out_specs=(VMEM,) * 3,
        scratch_shapes=[
            pltpu.VMEM((samples, hid), BF16),
            pltpu.VMEM((samples, hid // 2), BF16),
            pltpu.VMEM((pieces, 4, chunk, width), F32),
            pltpu.VMEM((pieces, 6, chunk // 2, width), F32),
            pltpu.VMEM((pieces, 6, tile // 2, width), F32),
            pltpu.VMEM((SPLITS, tile, 2 * width), F32),
            pltpu.VMEM((SPLITS, nz - 1, band, 2 * width), F32),
            pltpu.VMEM((SPLITS, band, 2 * width), F32),
            pltpu.VMEM((SPLITS, band // 2, 2 * width), F32),
            pltpu.VMEM((lookups, 2 * LANES), BF16),
            pltpu.VMEM((features, samples), I32),
            pltpu.VMEM((half_hot, 2 * LANES), F32),
            pltpu.VMEM((half_hot, LANES), F32),
            pltpu.VMEM((nx - 1, hrx, LANES), F32),
            pltpu.VMEM((ny - 1, hry, LANES), F32),
            pltpu.VMEM((nz - 1, hrz, LANES), F32),
            pltpu.VMEM((features, samples), F32),
            pltpu.VMEM((features, samples), I32),
            pltpu.VMEM((lookups, 2 * LANES), BF16),
            pltpu.VMEM((samples, lookups), BF16),
            pltpu.VMEM((4, n_mp, n_dp // 4, deep, 2 * LANES), BF16),
            pltpu.VMEM((4, n_mp, n_dp // 4, deep, 2 * LANES), BF16),
            pltpu.VMEM((4, n_dp // 4, n_mp, deep, 2 * LANES), BF16),
            pltpu.VMEM((devices, LANES), F32),
            pltpu.VMEM((n_mp, n_dp, LANES), F32),
            pltpu.VMEM((n_dp, n_mp, LANES), F32),
            pltpu.VMEM((n_dp, n_mp, LANES), F32),
            pltpu.VMEM((devices * deep // LANES, 2 * LANES), I32),
            pltpu.VMEM((group_slots, 2 * LANES), BF16),
            pltpu.VMEM((256, group_slots), BF16),
            dma((n_copies,)), dma((n_copies,)),
            dma((4, n_mp)), dma((4, n_mp)),
            dma((4, n_dp // 4)), dma((4, n_dp // 4)),
            dma((n_mp,)), dma((n_mp,)),
            dma((n_dp,)), dma((n_dp,)),
        ],
        compiler_params=pltpu.CompilerParams(
            vmem_limit_bytes=58 << 20, collective_id=0, has_side_effects=True
        ),
        name="step",
    )(
        pooled_in, out_grad, pooled_grad, hot_ids.T, cold_owner.T, cold_rows.T
    )

    steps = STEPS
    whole = lambda *shape: pl.BlockSpec(shape, lambda m: (0,) * len(shape))
    hot_block = pl.BlockSpec((hot // steps, LANES), lambda m: (m, 0))
    cold_block = pl.BlockSpec((2, rows // 2 // steps, LANES), lambda m: (0, m, 0))
    weight = whole(*mlp_weight.shape)
    hot_line, cold_line = whole(hot // LANES, LANES), whole(rows // LANES, LANES)
    new_weight, new_mlp_accum, new_hot, new_hot_accum, new_cold, new_cold_accum = pl.pallas_call(
        update_kernel,
        grid=(steps,),
        out_shape=(
            jax.ShapeDtypeStruct(mlp_weight.shape, F32),
            jax.ShapeDtypeStruct(mlp_accum.shape, F32),
            jax.ShapeDtypeStruct(hot_table.shape, F32),
            jax.ShapeDtypeStruct((hot // LANES, LANES), F32),
            jax.ShapeDtypeStruct((2, rows // 2, LANES), F32),
            jax.ShapeDtypeStruct((rows // LANES, LANES), F32),
        ),
        in_specs=[
            weight, hot_block, pl.BlockSpec((rows // 2 // steps, 2 * LANES), lambda m: (m, 0)),
            weight, weight, hot_block, hot_line, cold_block, cold_line,
        ],
        out_specs=(weight, weight, hot_block, hot_line, cold_block, cold_line),
        name="update",
    )(
        weight_grad, hot_grad, cold_grad, mlp_weight, mlp_accum,
        hot_table, hot_accum.reshape(hot // LANES, LANES),
        cold_table.reshape(2, rows // 2, LANES), cold_accum.reshape(rows // LANES, LANES),
    )
    return (
        new_weight,
        new_mlp_accum,
        new_hot,
        new_hot_accum.reshape(hot),
        new_cold.reshape(rows, LANES),
        new_cold_accum.reshape(rows),
    )


def solution(mesh):
    split = P(("dp", "mp"), None)
    nx = ny = 4
    nz = mesh.shape["mp"] // 2
    return jax.shard_map(
        functools.partial(shards, nx, ny, nz),
        mesh=mesh,
        in_specs=(split,) * 8 + (P(), P(), split, P(("dp", "mp"))),
        out_specs=(split, split, P(), P(), split, P(("dp", "mp"))),
        check_vma=False,
    )
```

time: 132 us -> 121 us (0.917); the launches traced: 132 us -> 118 us
  local copies, waits for them, and re-layouts: 10.8 us -> 0 us
  Pallas kernels: 120 us -> 118 us
    unnamed x14 -> x0, local copies, waits for them, and re-layouts: 10.8 us -> none
    pallas_call x1 -> x2, Pallas kernels: 120 us -> 118 us  [the longest x1 113 us: shards(): pl.pallas_call(functools.partial(step_kernel, nx, ny, nz, SPLITS, cap, fl...]
where the time goes in v3:
time: 121 us; the launch traced here: 118 us
  Pallas kernels  118 us (98%)
    pallas_call x1, Pallas kernels, shards(): pl.pallas_call(functools.partial(step_kernel, nx, ny, nz, SPLITS, cap, fl...  113 us
    pallas_call x1, Pallas kernels, shards(): pl.pallas_call(update_kernel, grid=(steps,), out_shape=(jax.ShapeDtypeStr...  5.06 us

profile of v3, /device:TPU:1, one launch (start us, length us, event | category | flops | bytes accessed | tf_op | source)
XLA Modules:
  0.0 118.4 jit_solution(14152314720086684587)
XLA Ops:
  0.6 112.6 %step.1 = (f32[8,2048]{1,0:T(8,128)}, f32[2048,128]{1,0:T(8,128)}, f32[2048,256]{1,0:T(8,128)}) custom-call(bf16[256,2048]{1,0:T(8,128)(2,1)} %x_ref.1, bf16[256,2048]{1,0:T(8,128)(2,1)} %g_ref.1, bf16[256,2048]{1,0:T(8,128)(2,1)} %pg_ref.1, s32[16,256]{1,0:T(8,128)} %bitcast.10, s32[1,4096]{1,0:T(1,128)} %bitcast.11, s32[16,256]{1,0:T(8,128)} %bitcast.12), custom_call_target="tpu_custom_call" | custom-call | tf_op jit(solution)/shard_map/step/pallas_call | solution.py:615
  113.2 5.1 %update.1 = (f32[8,2048]{1,0:T(8,128)}, f32[8,2048]{1,0:T(8,128)}, f32[2048,128]{1,0:T(8,128)}, f32[16,128]{1,0:T(8,128)}, f32[2,2048,128]{2,1,0:T(8,128)}, /*index=5*/f32[32,128]{1,0:T(8,128)}) custom-call(f32[8,2048]{1,0:T(8,128)} %get-tuple-element.15.wg_ref, f32[2048,128]{1,0:T(8,128)} %get-tuple-element.16.hot_ref, ...), custom_call_target="tpu_custom_call" | custom-call | tf_op jit(solution)/shard_map/update/pallas_call | solution.py:675

commit v4 on v3

--- a/solution.py
+++ b/solution.py
@@ -20,7 +20,7 @@
 STEPS = 2
 
 PLAN = (
-    ("cores",), ("far", 0), ("far", 1), ("near", 0), ("near", 1), ("bucket", 0),
+    ("bucket", 0), ("cores",), ("far", 0), ("far", 1), ("near", 0), ("near", 1),
     ("far", 2), ("far", 3), ("near", 2), ("near", 3), ("bucket", 1), ("bucket", 2),
     ("own", 0), ("own", 1), ("own", 2), ("own", 3), ("join", 0), ("join", 1), ("bucket", 3), ("join", 2), ("join", 3),
     ("numbers_on",), ("hot_product",), ("forward", 0), ("numbers_in",), ("hot_scatter", "x"), ("forward", 1),

time: 121 us -> 123 us (1.017); the launches traced: 118 us -> 122 us
  Pallas kernels: 118 us -> 121 us
    pallas_call x1, Pallas kernels: 113 us -> 116 us  [shards(): pl.pallas_call(functools.partial(step_kernel, nx, ny, nz, SPLITS, cap, fl...]
where the time goes in v4:
time: 123 us; the launch traced here: 122 us
  Pallas kernels  121 us (98%)
    pallas_call x1, Pallas kernels, shards(): pl.pallas_call(functools.partial(step_kernel, nx, ny, nz, SPLITS, cap, fl...  116 us
    pallas_call x1, Pallas kernels, shards(): pl.pallas_call(update_kernel, grid=(steps,), out_shape=(jax.ShapeDtypeStr...  5.06 us

profile of v4, /device:TPU:1, one launch (start us, length us, event | category | flops | bytes accessed | tf_op | source)
XLA Modules:
  0.0 121.7 jit_solution(2678732566076848906)
XLA Ops:
  0.6 115.8 %step.1 = (f32[8,2048]{1,0:T(8,128)}, f32[2048,128]{1,0:T(8,128)}, f32[2048,256]{1,0:T(8,128)}) custom-call(bf16[256,2048]{1,0:T(8,128)(2,1)} %x_ref.1, bf16[256,2048]{1,0:T(8,128)(2,1)} %g_ref.1, bf16[256,2048]{1,0:T(8,128)(2,1)} %pg_ref.1, s32[16,256]{1,0:T(8,128)} %bitcast.10, s32[1,4096]{1,0:T(1,128)} %bitcast.11, s32[16,256]{1,0:T(8,128)} %bitcast.12), custom_call_target="tpu_custom_call" | custom-call | tf_op jit(solution)/shard_map/step/pallas_call | solution.py:615
  116.5 5.1 %update.1 = (f32[8,2048]{1,0:T(8,128)}, f32[8,2048]{1,0:T(8,128)}, f32[2048,128]{1,0:T(8,128)}, f32[16,128]{1,0:T(8,128)}, f32[2,2048,128]{2,1,0:T(8,128)}, /*index=5*/f32[32,128]{1,0:T(8,128)}) custom-call(f32[8,2048]{1,0:T(8,128)} %get-tuple-element.15.wg_ref, f32[2048,128]{1,0:T(8,128)} %get-tuple-element.16.hot_ref, ...), custom_call_target="tpu_custom_call" | custom-call | tf_op jit(solution)/shard_map/update/pallas_call | solution.py:675
